TPU v7x, 32 devices: a whole 2x2x4 slice. The times are simulated.
32 devices in a mesh: shard: 8 (over z, core), ctx: 2 (over x), tp: 2 (over y).
Axes of the slice: x: 2, y: 2, z: 4, core: 2. Of those that a mesh axis runs over, the one named last changes fastest.
Arguments:
- tokens: bfloat16 [16, 1032, 1024], P('shard', 'ctx'), may hold values from -6 to 6
- cotangent: bfloat16 [16, 1032, 1024], P('shard', 'ctx'), may hold values from -6 to 6
- valid_tokens: int32 [16, 1032], P('shard'), may hold values from 0 to 1, as said below
- places: int32 [2, 16, 1032], P(None, 'shard', 'ctx'), may hold values from 0 to 31, as said below
- qkv_weight: bfloat16 [3, 1024, 1024], P(None, 'shard', 'tp'), may hold values from -0.1875 to 0.1875
- head_biases: bfloat16 [3, 16, 64], P(None, 'tp', 'shard'), may hold values from -1.1953125 to 1.1953125
- head_gain: bfloat16 [16, 64], P('tp', 'shard'), may hold values from 0.5 to 1.5
- out_weight: bfloat16 [1024, 1024], P('tp', 'shard'), may hold values from -0.1875 to 0.1875
- norm_gains: bfloat16 [2, 1024], P(None, 'shard'), may hold values from 0.5 to 1.5
- width_biases: bfloat16 [4, 1024], P(None, 'shard'), may hold values from -1.1953125 to 1.1953125
- gate_up: bfloat16 [2, 1024, 2730], P(None, 'shard', 'tp'), may hold values from -0.1875 to 0.1875
- hidden_biases: bfloat16 [3, 2730], P(None, 'tp'), may hold values from -1.1953125 to 1.1953125
- hidden_gain: bfloat16 [2730], P('tp'), may hold values from 0.5 to 1.5
- down_weight: bfloat16 [2730, 1024], P('tp', 'shard'), may hold values from -0.109375 to 0.109375
Outputs:
- output: bfloat16 [16, 1032, 1024], P('shard', 'ctx')
- tokens_grad: float32 [16, 1032, 1024], P('shard', 'ctx')
- qkv_grad: float32 [3, 1024, 1024], P(None, 'shard', 'tp')
- head_biases_grad: float32 [3, 16, 64], P(None, 'tp', 'shard')
- head_gain_grad: float32 [16, 64], P('tp', 'shard')
- out_weight_grad: float32 [1024, 1024], P('tp', 'shard')
- norm_gains_grad: float32 [2, 1024], P(None, 'shard')
- width_biases_grad: float32 [4, 1024], P(None, 'shard')
- gate_up_grad: float32 [2, 1024, 2730], P(None, 'shard', 'tp')
- hidden_biases_grad: float32 [3, 2730], P(None, 'tp')
- hidden_gain_grad: float32 [2730], P('tp')
- down_weight_grad: float32 [2730, 1024], P('tp', 'shard')
Inputs may be any that keep to these rules, and one draw needn't show every extreme that they name: `valid_tokens`: valid slots of each image form a prefix: the class token at slot 0 and 32 * w patch tokens after it, where w is 31 or 32; among the 2 images of each index of shard, one has w = 32. `places`: for a valid slot t >= 1 of an image with w columns the row is (t - 1) // w and the column (t - 1) % w; slot 0 and padding slots hold 0 and 0.
All inputs are finite; a program needn't handle non-finite values.
Results may differ from a plain program's by a relative error of at most 0.02.
Values may be sent and summed in bfloat16 or wider, within the bound.
A program may use at most 256 MiB of HBM per device.

v0:
```python
import math

import jax
import jax.numpy as jnp
from jax import lax
from jax.sharding import PartitionSpec as P

FF = 2730


EPS = 1e-06


def standardize(values):
    average = jnp.mean(values, axis=-1, keepdims=True)
    centred = values - average
    spread = lax.rsqrt(jnp.mean(centred * centred, axis=-1, keepdims=True) + EPS)
    return (centred * spread, spread)


def norm_back(grad_hat, normed, spread):
    mean_one = jnp.mean(grad_hat, axis=-1, keepdims=True)
    mean_two = jnp.mean(grad_hat * normed, axis=-1, keepdims=True)
    return (grad_hat - mean_one - normed * mean_two) * spread


def angle_table(row_ids, col_ids, head_size):
    quarter = head_size // 4
    frequency = 10000.0 ** (-jnp.arange(quarter, dtype=jnp.float32) / quarter)
    row_part = row_ids.astype(jnp.float32)[:, None] * frequency[None, :]
    col_part = col_ids.astype(jnp.float32)[:, None] * frequency[None, :]
    return jnp.concatenate([row_part, row_part, col_part, col_part], axis=1)


def turn_half(values):
    quarter = values.shape[-1] // 4
    part_one = values[..., :quarter]
    part_two = values[..., quarter : 2 * quarter]
    part_three = values[..., 2 * quarter : 3 * quarter]
    part_four = values[..., 3 * quarter :]
    return jnp.concatenate([-part_two, part_one, -part_four, part_three], axis=-1)


def rotate(values, angles):
    return values * jnp.cos(angles)[None, :, :] + turn_half(values) * jnp.sin(angles)[None, :, :]


def unrotate(values, angles):
    return values * jnp.cos(angles)[None, :, :] - turn_half(values) * jnp.sin(angles)[None, :, :]


def head_major(values, heads, head_size):
    return values.reshape(values.shape[0], heads, head_size).transpose(1, 0, 2)


def column_sum(values):
    return jnp.sum(values.astype(jnp.float32), axis=0)


def per_device(
    tokens,
    cotangent,
    valid_tokens,
    places,
    qkv_weight,
    head_biases,
    head_gain,
    out_weight,
    norm_gains,
    width_biases,
    gate_up,
    hidden_biases,
    hidden_gain,
    down_weight,
):
    micro = tokens.shape[0]
    width = tokens.shape[2]
    local_dim = qkv_weight.shape[2]
    local_heads = head_biases.shape[1]
    head_size = local_dim // local_heads
    local_hidden = hidden_gain.shape[0]
    score_scale = 1.0 / math.sqrt(head_size)
    f32 = jnp.float32
    bf16 = jnp.bfloat16

    def one_batch(batch_idx, carried):
        gathered = (
            lax.all_gather(qkv_weight, "shard", axis=1, tiled=True),
            lax.all_gather(head_biases, "shard", axis=2, tiled=True),
            lax.all_gather(head_gain, "shard", axis=1, tiled=True),
            lax.all_gather(out_weight, "shard", axis=1, tiled=True),
            lax.all_gather(norm_gains, "shard", axis=1, tiled=True),
            lax.all_gather(width_biases, "shard", axis=1, tiled=True),
            lax.all_gather(gate_up, "shard", axis=1, tiled=True),
            lax.all_gather(down_weight, "shard", axis=1, tiled=True),
        )
        qkv_full, head_bias, head_scale, out_full, norm_scale, width_bias, gate_full, down_full = (
            gathered
        )
        head_bias_f = head_bias.astype(f32)
        head_scale_f = head_scale.astype(f32)[:, None, :]
        norm_scale = norm_scale.astype(f32)
        width_bias = width_bias.astype(f32)
        hidden_bias = hidden_biases.astype(f32)
        hidden_scale = hidden_gain.astype(f32)
        out_heads = out_full.reshape(local_heads, head_size, width)
        token_rows = lax.dynamic_index_in_dim(tokens, batch_idx, 0, keepdims=False).astype(f32)
        cot_rows = lax.dynamic_index_in_dim(cotangent, batch_idx, 0, keepdims=False).astype(f32)
        valid_row = lax.dynamic_index_in_dim(valid_tokens, batch_idx, 0, keepdims=False) > 0
        row_ids = lax.dynamic_index_in_dim(places[0], batch_idx, 0, keepdims=False)
        col_ids = lax.dynamic_index_in_dim(places[1], batch_idx, 0, keepdims=False)
        angles = angle_table(row_ids, col_ids, head_size)
        normed_one, spread_one = standardize(token_rows)
        first_in = (normed_one * norm_scale[0] + width_bias[0]).astype(bf16)
        query_flat = jnp.dot(first_in, qkv_full[0], preferred_element_type=f32)
        key_flat = jnp.dot(first_in, qkv_full[1], preferred_element_type=f32)
        value_flat = jnp.dot(first_in, qkv_full[2], preferred_element_type=f32)
        query_pre = head_major(query_flat, local_heads, head_size) + head_bias_f[0][:, None, :]
        key_pre = head_major(key_flat, local_heads, head_size)
        value_local = (
            head_major(value_flat, local_heads, head_size) + head_bias_f[1][:, None, :]
        ).astype(bf16)
        queries = rotate(query_pre, angles).astype(bf16)
        key_local = rotate(key_pre, angles).astype(bf16)
        key_heads, value_heads = (
            lax.all_gather(key_local, "ctx", axis=1, tiled=True),
            lax.all_gather(value_local, "ctx", axis=1, tiled=True),
        )

        def score_block():
            raw = (
                jnp.einsum("htd,hsd->hts", queries, key_heads, preferred_element_type=f32)
                * score_scale
            )
            return jnp.where(valid_row[None, None, :], raw, -1e30)

        scores = score_block()
        row_top = jnp.max(scores, axis=-1, keepdims=True)
        row_total = jnp.sum(jnp.exp(scores - row_top), axis=-1, keepdims=True)
        soft_low = (jnp.exp(scores - row_top) / row_total).astype(bf16)
        mixed = jnp.einsum("hts,hsd->htd", soft_low, value_heads, preferred_element_type=f32)
        mix_sums = lax.psum(
            (
                jnp.sum(mixed, axis=(0, 2), keepdims=True),
                jnp.sum(mixed * mixed, axis=(0, 2), keepdims=True),
            ),
            "tp",
        )
        mix_mean = mix_sums[0] / width
        spread_mix = lax.rsqrt(mix_sums[1] / width - mix_mean * mix_mean + EPS)
        mix_hat = (mixed - mix_mean) * spread_mix
        mix_in = (mix_hat * head_scale_f + head_bias_f[2][:, None, :]).astype(bf16)
        branch = lax.psum(
            jnp.einsum("htd,hdn->tn", mix_in, out_heads, preferred_element_type=f32), "tp"
        )
        resid = token_rows + (branch + width_bias[2])
        normed_two, spread_two = standardize(resid)
        second_in = (normed_two * norm_scale[1] + width_bias[1]).astype(bf16)
        gate_pre = jnp.dot(second_in, gate_full[0], preferred_element_type=f32) + hidden_bias[0]
        up_pre = jnp.dot(second_in, gate_full[1], preferred_element_type=f32) + hidden_bias[1]
        sigmoid_gate = jax.nn.sigmoid(gate_pre)
        silu_gate = gate_pre * sigmoid_gate
        hidden = silu_gate * up_pre
        hidden_sums = lax.psum(
            (
                jnp.sum(hidden, axis=-1, keepdims=True),
                jnp.sum(hidden * hidden, axis=-1, keepdims=True),
            ),
            "tp",
        )
        hidden_mean = hidden_sums[0] / FF
        spread_hid = lax.rsqrt(hidden_sums[1] / FF - hidden_mean * hidden_mean + EPS)
        hidden_hat = (hidden - hidden_mean) * spread_hid
        down_in = (hidden_hat * hidden_scale + hidden_bias[2]).astype(bf16)
        ffn_out = lax.psum(
            jnp.dot(down_in, down_full, preferred_element_type=f32).astype(jnp.bfloat16), "tp"
        ).astype(jnp.float32)
        result = (resid + (ffn_out + width_bias[3])).astype(bf16)
        d_ffn_low = cot_rows.astype(bf16)
        g_down = jnp.einsum("tf,td->fd", down_in, d_ffn_low, preferred_element_type=f32)
        d_down_in = jnp.einsum("td,fd->tf", d_ffn_low, down_full, preferred_element_type=f32)
        grad_hid = d_down_in * hidden_scale
        hid_back = lax.psum(
            (
                jnp.sum(grad_hid, axis=-1, keepdims=True),
                jnp.sum(grad_hid * hidden_hat, axis=-1, keepdims=True),
            ),
            "tp",
        )
        d_hidden = (grad_hid - hid_back[0] / FF - hidden_hat * (hid_back[1] / FF)) * spread_hid
        d_gate = (
            d_hidden * up_pre * sigmoid_gate * (1.0 + gate_pre * (1.0 - sigmoid_gate))
        ).astype(bf16)
        d_up = (d_hidden * silu_gate).astype(bf16)
        g_gate_one = jnp.einsum("td,tf->df", second_in, d_gate, preferred_element_type=f32)
        g_up_one = jnp.einsum("td,tf->df", second_in, d_up, preferred_element_type=f32)
        d_second_part = jnp.einsum(
            "tf,df->td", d_gate, gate_full[0], preferred_element_type=f32
        ) + jnp.einsum("tf,df->td", d_up, gate_full[1], preferred_element_type=f32)
        d_second = lax.psum(d_second_part, "tp")
        d_resid = cot_rows + norm_back(d_second * norm_scale[1], normed_two, spread_two)
        d_branch_low = d_resid.astype(bf16)
        g_out = jnp.einsum("htd,tn->hdn", mix_in, d_branch_low, preferred_element_type=f32).reshape(
            local_dim, width
        )
        d_mix_in = jnp.einsum("tn,hdn->htd", d_branch_low, out_heads, preferred_element_type=f32)
        grad_mix = d_mix_in * head_scale_f
        mix_back = lax.psum(
            (
                jnp.sum(grad_mix, axis=(0, 2), keepdims=True),
                jnp.sum(grad_mix * mix_hat, axis=(0, 2), keepdims=True),
            ),
            "tp",
        )
        d_mixed = (
            (grad_mix - mix_back[0] / width - mix_hat * (mix_back[1] / width)) * spread_mix
        ).astype(bf16)
        again = score_block()
        weights_soft = jnp.exp(again - row_top) / row_total
        d_soft = jnp.einsum("htd,hsd->hts", d_mixed, value_heads, preferred_element_type=f32)
        row_dot = jnp.sum(weights_soft * d_soft, axis=-1, keepdims=True)
        d_scores = (weights_soft * (d_soft - row_dot)).astype(bf16)
        d_query = (
            jnp.einsum("hts,hsd->htd", d_scores, key_heads, preferred_element_type=f32)
            * score_scale
        )
        soft_again = weights_soft.astype(bf16)
        d_key_all = (
            jnp.einsum("hts,htd->hsd", d_scores, queries, preferred_element_type=f32) * score_scale
        )
        d_value_all = jnp.einsum("hts,htd->hsd", soft_again, d_mixed, preferred_element_type=f32)
        d_key_heads, d_value_loc = (
            lax.psum_scatter(
                d_key_all.astype(jnp.bfloat16), "ctx", scatter_dimension=1, tiled=True
            ).astype(jnp.float32),
            lax.psum_scatter(
                d_value_all.astype(jnp.bfloat16), "ctx", scatter_dimension=1, tiled=True
            ).astype(jnp.float32),
        )
        d_query_low = unrotate(d_query, angles).astype(bf16)
        d_key_low = unrotate(d_key_heads, angles).astype(bf16)
        d_value_low = d_value_loc.astype(bf16)
        g_query = jnp.einsum(
            "tn,htd->nhd", first_in, d_query_low, preferred_element_type=f32
        ).reshape(width, local_dim)
        g_key = jnp.einsum("tn,htd->nhd", first_in, d_key_low, preferred_element_type=f32).reshape(
            width, local_dim
        )
        g_value = jnp.einsum(
            "tn,htd->nhd", first_in, d_value_low, preferred_element_type=f32
        ).reshape(width, local_dim)
        d_first_part = jnp.einsum(
            "htd,nhd->tn",
            d_query_low,
            qkv_full[0].reshape(width, local_heads, head_size),
            preferred_element_type=f32,
        )
        d_first_part = d_first_part + jnp.einsum(
            "htd,nhd->tn",
            d_key_low,
            qkv_full[1].reshape(width, local_heads, head_size),
            preferred_element_type=f32,
        )
        d_first_part = d_first_part + jnp.einsum(
            "htd,nhd->tn",
            d_value_low,
            qkv_full[2].reshape(width, local_heads, head_size),
            preferred_element_type=f32,
        )
        d_first = lax.psum(d_first_part.astype(jnp.bfloat16), "tp").astype(jnp.float32)
        d_tokens = d_resid + norm_back(d_first * norm_scale[0], normed_one, spread_one)
        g_head_bias = jnp.stack(
            [
                jnp.sum(d_query_low.astype(f32), axis=1),
                jnp.sum(d_value_low.astype(f32), axis=1),
                jnp.sum(d_mix_in, axis=1),
            ]
        )
        g_head_scale = jnp.sum(d_mix_in * mix_hat, axis=1)
        g_norm = jnp.stack([column_sum(d_first * normed_one), column_sum(d_second * normed_two)])
        g_width = jnp.stack(
            [
                column_sum(d_first),
                column_sum(d_second),
                column_sum(d_branch_low),
                column_sum(d_ffn_low),
            ]
        )
        g_hidden_bias = jnp.stack([column_sum(d_gate), column_sum(d_up), column_sum(d_down_in)])
        g_hidden_scale = column_sum(d_down_in * hidden_hat)
        out_all = lax.dynamic_update_index_in_dim(carried[0], result, batch_idx, 0)
        grad_all = lax.dynamic_update_index_in_dim(carried[1], d_tokens, batch_idx, 0)
        updates = (
            g_query,
            g_key,
            g_value,
            g_head_bias,
            g_head_scale,
            g_out,
            g_norm,
            g_width,
            g_gate_one,
            g_up_one,
            g_down,
            g_hidden_bias,
            g_hidden_scale,
        )
        return (
            out_all,
            grad_all,
            tuple((before + added for before, added in zip(carried[2], updates))),
        )

    zeros_acc = (
        jnp.zeros((width, local_dim), f32),
        jnp.zeros((width, local_dim), f32),
        jnp.zeros((width, local_dim), f32),
        jnp.zeros((3, local_heads, head_size), f32),
        jnp.zeros((local_heads, head_size), f32),
        jnp.zeros((local_dim, width), f32),
        jnp.zeros((2, width), f32),
        jnp.zeros((4, width), f32),
        jnp.zeros((width, local_hidden), f32),
        jnp.zeros((width, local_hidden), f32),
        jnp.zeros((local_hidden, width), f32),
        jnp.zeros((3, local_hidden), f32),
        jnp.zeros((local_hidden,), f32),
    )
    start = (jnp.zeros(tokens.shape, bf16), jnp.zeros(tokens.shape, f32), zeros_acc)
    out_all, grad_all, summed = lax.fori_loop(0, micro, one_batch, start)
    (
        acc_query,
        acc_key,
        acc_value,
        acc_head_bias,
        acc_head_scale,
        acc_out,
        acc_norm,
        acc_width,
        acc_gate_one,
        acc_up_one,
        acc_down,
        acc_hidden_bias,
        acc_hidden_scale,
    ) = summed
    acc_qkv = jnp.stack([acc_query, acc_key, acc_value])
    acc_gate = jnp.stack([acc_gate_one, acc_up_one])
    sharded = (
        acc_qkv,
        acc_head_bias,
        acc_head_scale,
        acc_out,
        acc_norm,
        acc_width,
        acc_gate,
        acc_down,
    )
    hidden_done = lax.psum((acc_hidden_bias, acc_hidden_scale), ("shard", "ctx"))
    return (
        out_all,
        grad_all,
        lax.psum_scatter(
            lax.psum(sharded[0].astype(jnp.bfloat16), "ctx"),
            "shard",
            scatter_dimension=1,
            tiled=True,
        ).astype(jnp.float32),
        lax.psum_scatter(
            lax.psum(sharded[1].astype(jnp.bfloat16), "ctx"),
            "shard",
            scatter_dimension=2,
            tiled=True,
        ).astype(jnp.float32),
        lax.psum_scatter(
            lax.psum(sharded[2].astype(jnp.bfloat16), "ctx"),
            "shard",
            scatter_dimension=1,
            tiled=True,
        ).astype(jnp.float32),
        lax.psum_scatter(
            lax.psum(sharded[3].astype(jnp.bfloat16), "ctx"),
            "shard",
            scatter_dimension=1,
            tiled=True,
        ).astype(jnp.float32),
        lax.psum_scatter(
            lax.psum(sharded[4].astype(jnp.bfloat16), "ctx"),
            "shard",
            scatter_dimension=1,
            tiled=True,
        ).astype(jnp.float32),
        lax.psum_scatter(
            lax.psum(sharded[5].astype(jnp.bfloat16), "ctx"),
            "shard",
            scatter_dimension=1,
            tiled=True,
        ).astype(jnp.float32),
        lax.psum_scatter(
            lax.psum(sharded[6].astype(jnp.bfloat16), "ctx"),
            "shard",
            scatter_dimension=1,
            tiled=True,
        ).astype(jnp.float32),
        hidden_done[0],
        hidden_done[1],
        lax.psum_scatter(
            lax.psum(sharded[7].astype(jnp.bfloat16), "ctx"),
            "shard",
            scatter_dimension=1,
            tiled=True,
        ).astype(jnp.float32),
    )


def solution(mesh):
    return jax.shard_map(
        per_device,
        mesh=mesh,
        in_specs=(
            P("shard", "ctx", None),
            P("shard", "ctx", None),
            P("shard", None),
            P(None, "shard", "ctx"),
            P(None, "shard", "tp"),
            P(None, "tp", "shard"),
            P("tp", "shard"),
            P("tp", "shard"),
            P(None, "shard"),
            P(None, "shard"),
            P(None, "shard", "tp"),
            P(None, "tp"),
            P("tp"),
            P("tp", "shard"),
        ),
        out_specs=(
            P("shard", "ctx", None),
            P("shard", "ctx", None),
            P(None, "shard", "tp"),
            P(None, "tp", "shard"),
            P("tp", "shard"),
            P("tp", "shard"),
            P(None, "shard"),
            P(None, "shard"),
            P(None, "shard", "tp"),
            P(None, "tp"),
            P("tp"),
            P("tp", "shard"),
        ),
        check_vma=False,
    )
```

profile of v0, /device:TPU:0, one launch (start us, length us, event | category | flops | bytes accessed | tf_op | source)
XLA Modules:
  0.0 1650.0 jit_solution(5967282522983737245)
XLA Ops:
  18.4 1315.3 %while.42 = (s32[]{:T(128)}, bf16[2,516,1024]{2,1,0:T(8,128)(2,1)}, f32[2,516,1024]{2,0,1:T(2,128)}, f32[1024,512]{1,0:T(8,128)}, f32[1024,512]{1,0:T(8,128)}, /...) while((s32[]{:T(128)}, bf16[2,516,1024]{2,1,0:T(8,128)(2,1)}, ...), condition=%wide.region_48.49_spmd.clone, body=%wide.region_0.48_spmd.clone.sunk | while | flops 24057417728 | bytes 724958848 | solution.py:330
  19.4 15.9 all_gather.92
  79.3 13.2 all_gather.97
  108.5 31.0 %all-gather.13.cloned.1.call-done = bf16[8,1032,64]{2,0,1:T(8,128)(2,1)} async-done(((bf16[8,516,64]{2,0,1:T(8,128)(2,1)}), bf16[8,1032,64]{2,0,1:T(8,128)(2,1)}) %all-gather.13.cloned.1.call-update) | async-done | bytes 1056784 | tf_op jit(solution)/shard_map/while/body/eval_jaxpr/all_gather | solution.py:126
  173.3 61.1 %all-reduce.34.cloned.1.call-done = f32[516,1024]{1,0:T(8,128)} async-done(((f32[516,1024]{1,0:T(8,128)}), f32[516,1024]{1,0:T(8,128)}) %all-reduce.34.cloned.1.call-update) | async-done | bytes 2113552 | tf_op jit(solution)/shard_map/while/body/eval_jaxpr/psum | solution.py:153
  237.5 58.6 %all-gather.17.cloned.1.call-done = bf16[2,1024,1365]{1,2,0:T(8,128)(2,1)} async-done(((bf16[2,128,1365]{1,2,0:T(8,128)(2,1)}), bf16[2,1024,1365]{1,2,0:T(8,128)(2,1)}) %all-gather.17.cloned.1.call-update) | async-done | bytes 5591056 | tf_op jit(solution)/shard_map/while/body/eval_jaxpr/all_gather | solution.py:94
  309.9 22.4 %all-gather.15.cloned.1.call-done = bf16[1365,1024]{1,0:T(8,128)(2,1)} async-done(((bf16[1365,128]{1,0:T(8,128)(2,1)}), bf16[1365,1024]{1,0:T(8,128)(2,1)}) %all-gather.15.cloned.1.call-update) | async-done | bytes 2795536 | tf_op jit(solution)/shard_map/while/body/eval_jaxpr/all_gather | solution.py:95
  374.7 45.7 %all-reduce.36.cloned.1.call-done = f32[516,1024]{1,0:T(8,128)} async-done(((f32[516,1024]{1,0:T(8,128)}), f32[516,1024]{1,0:T(8,128)}) %all-reduce.36.cloned.1.call-update) | async-done | bytes 2113552 | tf_op jit(solution)/shard_map/while/body/eval_jaxpr/psum | solution.py:200
  445.5 13.0 multiply_reduce_fusion.40
  458.5 17.4 %multiply_convert_fusion.9 = bf16[8,516,1032]{2,1,0:T(8,128)(2,1)} fusion(f32[8,516,1032]{2,1,0:T(8,128)} %get-tuple-element.1306, f32[8,516]{1,0:T(8,128)S(1)} %get-tuple-element.1307, f32[8,516]{1,0:T(8,128)S(1)} %get-tuple-element.1265, f32[8,516,1032]{2,1,0:T(8,128)} %get-tuple-element.1289), kind=kLoop, calls=%fused_computation.2.clone.1 | loop fusion | flops 17040384 | bytes 42633984 | tf_op jit(solution)/shard_map/while/body/eval_jaxpr/convert_element_type | solution.py:222
  499.9 51.7 %all-reduce.38.cloned.1.call-done = (bf16[8,1032,64]{1,2,0:T(8,128)(2,1)}, bf16[8,1032,64]{1,2,0:T(8,128)(2,1)}) async-done(((bf16[8,1032,64]{1,2,0:T(8,128)(2,1)}, bf16[8,1032,64]{1,2,0:T(8,128)(2,1)}), (bf16[8,1032,64]{1,2,0:T(8,128)(2,1)}, bf16[8,1032,64]{1,2,0:T(8,128)(2,1)})) %all-reduce.38.cloned.1.call-update) | async-done | bytes 2113552 | tf_op jit(solution)/shard_map/while
  579.6 45.8 %all-reduce.40.cloned.1.call-done = (bf16[516,1024]{1,0:T(8,128)(2,1)}, bf16[516,1024]{1,0:T(8,128)(2,1)}) async-done(((bf16[516,1024]{1,0:T(8,128)(2,1)}, bf16[516,1024]{1,0:T(8,128)(2,1)}), (bf16[516,1024]{1,0:T(8,128)(2,1)}, bf16[516,1024]{1,0:T(8,128)(2,1)})) %all-reduce.40.cloned.1.call-update) | async-done | bytes 2113552 | tf_op jit(solution)/shard_map/while/body/eval_jaxpr/psum | solution.py:175
  634.0 37.1 %dynamic_update_slice.22 = f32[2,516,1024]{2,0,1:T(2,128)} dynamic-update-slice(f32[2,516,1024]{2,0,1:T(2,128)} %get-tuple-element.1380, f32[1,516,1024]{2,0,1:T(1,128)} %copy.113, s32[]{:T(128)S(6)} %copy.138, s32[]{:T(128)} %constant.173.clone.1..sunk, s32[]{:T(128)} %constant.173.clone.1..sunk) | dynamic-update-slice | bytes 4227076 | tf_op jit(solution)/shard_map/while/body/eval_jaxpr/jit(dynamic_update_index_in_dim)/dynamic_update_slice | solution.py:292
  674.5 14.3 all_gather.92
  733.4 12.7 all_gather.97
  761.1 31.4 %all-gather.13.cloned.1.call-done = bf16[8,1032,64]{2,0,1:T(8,128)(2,1)} async-done(((bf16[8,516,64]{2,0,1:T(8,128)(2,1)}), bf16[8,1032,64]{2,0,1:T(8,128)(2,1)}) %all-gather.13.cloned.1.call-update) | async-done | bytes 1056784 | tf_op jit(solution)/shard_map/while/body/eval_jaxpr/all_gather | solution.py:126
  826.2 61.3 %all-reduce.34.cloned.1.call-done = f32[516,1024]{1,0:T(8,128)} async-done(((f32[516,1024]{1,0:T(8,128)}), f32[516,1024]{1,0:T(8,128)}) %all-reduce.34.cloned.1.call-update) | async-done | bytes 2113552 | tf_op jit(solution)/shard_map/while/body/eval_jaxpr/psum | solution.py:153
  890.5 58.6 %all-gather.17.cloned.1.call-done = bf16[2,1024,1365]{1,2,0:T(8,128)(2,1)} async-done(((bf16[2,128,1365]{1,2,0:T(8,128)(2,1)}), bf16[2,1024,1365]{1,2,0:T(8,128)(2,1)}) %all-gather.17.cloned.1.call-update) | async-done | bytes 5591056 | tf_op jit(solution)/shard_map/while/body/eval_jaxpr/all_gather | solution.py:94
  962.9 22.3 %all-gather.15.cloned.1.call-done = bf16[1365,1024]{1,0:T(8,128)(2,1)} async-done(((bf16[1365,128]{1,0:T(8,128)(2,1)}), bf16[1365,1024]{1,0:T(8,128)(2,1)}) %all-gather.15.cloned.1.call-update) | async-done | bytes 2795536 | tf_op jit(solution)/shard_map/while/body/eval_jaxpr/all_gather | solution.py:95
  1034.4 38.9 %all-reduce.36.cloned.1.call-done = f32[516,1024]{1,0:T(8,128)} async-done(((f32[516,1024]{1,0:T(8,128)}), f32[516,1024]{1,0:T(8,128)}) %all-reduce.36.cloned.1.call-update) | async-done | bytes 2113552 | tf_op jit(solution)/shard_map/while/body/eval_jaxpr/psum | solution.py:200
  1098.1 13.0 multiply_reduce_fusion.40
  1111.1 17.4 %multiply_convert_fusion.9 = bf16[8,516,1032]{2,1,0:T(8,128)(2,1)} fusion(f32[8,516,1032]{2,1,0:T(8,128)} %get-tuple-element.1306, f32[8,516]{1,0:T(8,128)S(1)} %get-tuple-element.1307, f32[8,516]{1,0:T(8,128)S(1)} %get-tuple-element.1265, f32[8,516,1032]{2,1,0:T(8,128)} %get-tuple-element.1289), kind=kLoop, calls=%fused_computation.2.clone.1 | loop fusion | flops 17040384 | bytes 42633984 | tf_op jit(solution)/shard_map/while/body/eval_jaxpr/convert_element_type | solution.py:222
  1154.3 50.0 %all-reduce.38.cloned.1.call-done = (bf16[8,1032,64]{1,2,0:T(8,128)(2,1)}, bf16[8,1032,64]{1,2,0:T(8,128)(2,1)}) async-done(((bf16[8,1032,64]{1,2,0:T(8,128)(2,1)}, bf16[8,1032,64]{1,2,0:T(8,128)(2,1)}), (bf16[8,1032,64]{1,2,0:T(8,128)(2,1)}, bf16[8,1032,64]{1,2,0:T(8,128)(2,1)})) %all-reduce.38.cloned.1.call-update) | async-done | bytes 2113552 | tf_op jit(solution)/shard_map/while
  1233.1 44.9 %all-reduce.40.cloned.1.call-done = (bf16[516,1024]{1,0:T(8,128)(2,1)}, bf16[516,1024]{1,0:T(8,128)(2,1)}) async-done(((bf16[516,1024]{1,0:T(8,128)(2,1)}, bf16[516,1024]{1,0:T(8,128)(2,1)}), (bf16[516,1024]{1,0:T(8,128)(2,1)}, bf16[516,1024]{1,0:T(8,128)(2,1)})) %all-reduce.40.cloned.1.call-update) | async-done | bytes 2113552 | tf_op jit(solution)/shard_map/while/body/eval_jaxpr/psum | solution.py:175
  1286.7 37.1 %dynamic_update_slice.22 = f32[2,516,1024]{2,0,1:T(2,128)} dynamic-update-slice(f32[2,516,1024]{2,0,1:T(2,128)} %get-tuple-element.1380, f32[1,516,1024]{2,0,1:T(1,128)} %copy.113, s32[]{:T(128)S(6)} %copy.138, s32[]{:T(128)} %constant.173.clone.1..sunk, s32[]{:T(128)} %constant.173.clone.1..sunk) | dynamic-update-slice | bytes 4227076 | tf_op jit(solution)/shard_map/while/body/eval_jaxpr/jit(dynamic_update_index_in_dim)/dynamic_update_slice | solution.py:292
  1351.0 15.0 copy.86
  1389.2 18.9 %reduce-scatter.31.cloned.1.call-done = bf16[128,1365]{1,0:T(8,128)(2,1)} async-done(((bf16[1024,1365]{1,0:T(8,128)(2,1)}), bf16[128,1365]{1,0:T(8,128)(2,1)}) %reduce-scatter.31.cloned.1.call-update) | async-done | bytes 349456
  1410.0 64.3 %reduce-scatter.29.cloned.1.call-done = bf16[128,2730]{1,0:T(8,128)(2,1)} async-done(((bf16[1024,2730]{1,0:T(8,128)(2,1)}), bf16[128,2730]{1,0:T(8,128)(2,1)}) %reduce-scatter.29.cloned.1.call-update) | async-done | bytes 698896
  1478.6 36.5 %reduce-scatter.21.cloned.1.call-done = bf16[3,128,512]{2,1,0:T(8,128)(2,1)} async-done(((bf16[3,1024,512]{2,1,0:T(8,128)(2,1)}), bf16[3,128,512]{2,1,0:T(8,128)(2,1)}) %reduce-scatter.21.cloned.1.call-update) | async-done | bytes 393232 | tf_op jit(solution)/shard_map/reduce_scatter | solution.py:362
  1520.0 15.2 all-reduce.11
  1535.2 60.0 %all-reduce.10 = (f32[3,1365]{1,0:T(4,128)}, f32[1365]{0:T(1024)}) all-reduce(f32[3,1365]{1,0:T(4,128)S(1)} %copy-done.57, f32[1365]{0:T(1024)} %get-tuple-element.1626), channel_id=1, replica_groups=mesh['shard'=8,'ctx'=2,'tp'=2] {'shard','ctx'}, use_global_device_ids=true, to_apply=%region_63.64 | all-reduce | flops 5460 | bytes 43680 | tf_op jit(solution)/shard_map/psum | solution.py:358
  1604.7 27.3 %all-reduce.32.cloned.1.call-done = (bf16[2,128,1365]{1,2,0:T(8,128)(2,1)}, bf16[3,128,512]{2,1,0:T(8,128)(2,1)}, bf16[512,128]{1,0:T(8,128)(2,1)}, bf16[1365,128]{1,0:T(8,128)(2,1)}) async-done(((bf16[2,128,1365]{1,2,0:T(8,128)(2,1)}, bf16[3,128,512]{2,1,0:T(8,128)(2,1)}, bf16[512,128]{1,0:T(8,128)(2,1)}, bf16[1365,128]{1,0:T(8,128)(2,1)}), (bf16[2,128,1365]{1,2,0:T(8,128)(2,1)}, ...) | async-done | bytes 1572624 | tf_op jit(solution)/shard_map/psum | solution.py:399
  (673 shorter events, 568.7 us)
Async XLA Ops:
  18.6 44.5 %all-gather.9.cloned.1.call-start = ((), (), s32[]{:S(2)}) async-start(), calls=%async_computation.14 | async-start | bytes 3538944 | tf_op jit(solution)/shard_map/while/body/eval_jaxpr/all_gather | solution.py:88
  19.4 84.6 %all-gather.11.cloned.1.call-start = ((), (), s32[]{:S(2)}) async-start(), calls=%async_computation.15 | async-start | bytes 3170304 | tf_op jit(solution)/shard_map/while/body/eval_jaxpr/all_gather | solution.py:127
  70.8 68.7 %all-gather.13.cloned.1.call-start = ((), (), s32[]{:S(2)}) async-start(), calls=%async_computation.16 | async-start | bytes 3170304 | tf_op jit(solution)/shard_map/while/body/eval_jaxpr/all_gather | solution.py:126
  78.6 88.5 %all-gather.7.cloned.1.call-start = ((), (), s32[]{:S(2)}) async-start(), calls=%async_computation.13 | async-start | bytes 1179648 | tf_op jit(solution)/shard_map/while/body/eval_jaxpr/all_gather | solution.py:91
  79.2 155.2 %all-reduce.34.cloned.1.call-start = ((), (), s32[]{:S(2)}) async-start(), calls=%async_computation.17 | async-start | bytes 4259840 | tf_op jit(solution)/shard_map/while/body/eval_jaxpr/psum | solution.py:153
  170.6 125.5 %all-gather.17.cloned.1.call-start = ((), (), s32[]{:S(2)}) async-start(), calls=%async_computation.19 | async-start | bytes 6303744 | tf_op jit(solution)/shard_map/while/body/eval_jaxpr/all_gather | solution.py:94
  171.2 161.1 %all-gather.15.cloned.1.call-start = ((), (), s32[]{:S(2)}) async-start(), calls=%async_computation.18 | async-start | bytes 3151872 | tf_op jit(solution)/shard_map/while/body/eval_jaxpr/all_gather | solution.py:95
  171.9 248.5 %all-reduce.36.cloned.1.call-start = ((), (), s32[]{:S(2)}) async-start(), calls=%async_computation.20 | async-start | bytes 4259840 | tf_op jit(solution)/shard_map/while/body/eval_jaxpr/psum | solution.py:200
  173.3 185.9 %copy-start.72 = (f32[1365]{0:T(1024)}, f32[1365]{0:T(1024)S(1)}, u32[]{:S(2)}) copy-start(f32[1365]{0:T(1024)S(1)} %get-tuple-element.1282) | copy-start | bytes 16384 | tf_op jit(solution)/shard_map/while
  358.3 193.3 %all-reduce.38.cloned.1.call-start = ((), (), s32[]{:S(2)}) async-start(), calls=%async_computation.21 | async-start | bytes 4718592 | tf_op jit(solution)/shard_map/while
  482.6 142.8 %all-reduce.40.cloned.1.call-start = ((), (), s32[]{:S(2)}) async-start(), calls=%async_computation.22 | async-start | bytes 4259840 | tf_op jit(solution)/shard_map/while/body/eval_jaxpr/psum | solution.py:175
  673.7 43.6 %all-gather.9.cloned.1.call-start = ((), (), s32[]{:S(2)}) async-start(), calls=%async_computation.14 | async-start | bytes 3538944 | tf_op jit(solution)/shard_map/while/body/eval_jaxpr/all_gather | solution.py:88
  674.4 82.6 %all-gather.11.cloned.1.call-start = ((), (), s32[]{:S(2)}) async-start(), calls=%async_computation.15 | async-start | bytes 3170304 | tf_op jit(solution)/shard_map/while/body/eval_jaxpr/all_gather | solution.py:127
  724.9 67.6 %all-gather.13.cloned.1.call-start = ((), (), s32[]{:S(2)}) async-start(), calls=%async_computation.16 | async-start | bytes 3170304 | tf_op jit(solution)/shard_map/while/body/eval_jaxpr/all_gather | solution.py:126
  732.7 87.4 %all-gather.7.cloned.1.call-start = ((), (), s32[]{:S(2)}) async-start(), calls=%async_computation.13 | async-start | bytes 1179648 | tf_op jit(solution)/shard_map/while/body/eval_jaxpr/all_gather | solution.py:91
  733.3 154.2 %all-reduce.34.cloned.1.call-start = ((), (), s32[]{:S(2)}) async-start(), calls=%async_computation.17 | async-start | bytes 4259840 | tf_op jit(solution)/shard_map/while/body/eval_jaxpr/psum | solution.py:153
  823.6 125.5 %all-gather.17.cloned.1.call-start = ((), (), s32[]{:S(2)}) async-start(), calls=%async_computation.19 | async-start | bytes 6303744 | tf_op jit(solution)/shard_map/while/body/eval_jaxpr/all_gather | solution.py:94
  824.2 161.0 %all-gather.15.cloned.1.call-start = ((), (), s32[]{:S(2)}) async-start(), calls=%async_computation.18 | async-start | bytes 3151872 | tf_op jit(solution)/shard_map/while/body/eval_jaxpr/all_gather | solution.py:95
  824.8 248.5 %all-reduce.36.cloned.1.call-start = ((), (), s32[]{:S(2)}) async-start(), calls=%async_computation.20 | async-start | bytes 4259840 | tf_op jit(solution)/shard_map/while/body/eval_jaxpr/psum | solution.py:200
  826.2 186.8 %copy-start.72 = (f32[1365]{0:T(1024)}, f32[1365]{0:T(1024)S(1)}, u32[]{:S(2)}) copy-start(f32[1365]{0:T(1024)S(1)} %get-tuple-element.1282) | copy-start | bytes 16384 | tf_op jit(solution)/shard_map/while
  1011.2 193.0 %all-reduce.38.cloned.1.call-start = ((), (), s32[]{:S(2)}) async-start(), calls=%async_computation.21 | async-start | bytes 4718592 | tf_op jit(solution)/shard_map/while
  1135.3 142.8 %all-reduce.40.cloned.1.call-start = ((), (), s32[]{:S(2)}) async-start(), calls=%async_computation.22 | async-start | bytes 4259840 | tf_op jit(solution)/shard_map/while/body/eval_jaxpr/psum | solution.py:175
  1333.7 53.9 %reduce-scatter.23.cloned.1.call-start = ((), (), s32[]{:S(2)}) async-start(), calls=%async_computation.7 | async-start | bytes 1179648
  1336.9 71.3 %reduce-scatter.31.cloned.1.call-start = ((), (), s32[]{:S(2)}) async-start(), calls=%async_computation.11 | async-start | bytes 3244032
  1342.8 131.5 %reduce-scatter.29.cloned.1.call-start = ((), (), s32[]{:S(2)}) async-start(), calls=%async_computation.10 | async-start | bytes 6488064
  1378.7 136.4 %reduce-scatter.21.cloned.1.call-start = ((), (), s32[]{:S(2)}) async-start(), calls=%async_computation.6 | async-start | bytes 3538944 | tf_op jit(solution)/shard_map/reduce_scatter | solution.py:362
  1384.9 210.4 %reduce-scatter.25.cloned.1.call-start = ((), (), s32[]{:S(2)}) async-start(), calls=%async_computation.8 | async-start | bytes 294912
  1386.5 209.7 %reduce-scatter.27.cloned.1.call-start = ((), (), s32[]{:S(2)}) async-start(), calls=%async_computation.9 | async-start | bytes 294912
  1387.5 244.5 %all-reduce.32.cloned.1.call-start = ((), (), s32[]{:S(2)}) async-start(), calls=%async_computation.12 | async-start | bytes 3149824 | tf_op jit(solution)/shard_map/psum | solution.py:399
  1410.0 105.2 %copy-start.76 = (f32[8,64]{1,0:T(8,128)S(1)}, f32[8,64]{1,0:T(8,128)}, u32[]{:S(2)}) copy-start(f32[8,64]{1,0:T(8,128)} %get-tuple-element.1618) | copy-start | bytes 6148
  1410.0 105.2 %copy-start.63 = (f32[3,8,64]{2,1,0:T(8,128)S(1)}, f32[3,8,64]{2,1,0:T(8,128)}, u32[]{:S(2)}) copy-start(f32[3,8,64]{2,1,0:T(8,128)} %get-tuple-element.1617) | copy-start | bytes 18436
  1410.0 105.2 %copy-start.41 = (bf16[2,516,1024]{2,1,0:T(8,128)(2,1)S(1)}, bf16[2,516,1024]{2,1,0:T(8,128)(2,1)}, u32[]{:S(2)}) copy-start(bf16[2,516,1024]{2,1,0:T(8,128)(2,1)} %get-tuple-element.1612) | copy-start | bytes 6340612
  (164 other events, 1207.6 us)
Sparse Core Ops, SparseCore 0:
  21.2 41.9 all-gather.8
  70.9 33.0 all-gather.10
  106.2 33.2 all-gather.12
  141.1 23.9 all-gather.6
  170.7 63.6 all-reduce.33
  236.5 59.4 all-gather.16
  297.7 34.5 all-gather.14
  358.4 61.9 all-reduce.35
  482.7 68.7 all-reduce.37
  561.5 63.8 all-reduce.39
  676.2 41.0 all-gather.8
  725.0 31.9 all-gather.10
  759.2 33.2 all-gather.12
  794.1 23.9 all-gather.6
  823.7 63.6 all-reduce.33
  889.6 59.4 all-gather.16
  950.6 34.5 all-gather.14
  1011.3 61.9 all-reduce.35
  1135.4 68.7 all-reduce.37
  1214.2 63.8 all-reduce.39
Sparse Core Ops, SparseCore 1:
  1337.0 32.2 reduce-scatter.22
  1371.5 36.6 reduce-scatter.30
  1410.3 64.0 reduce-scatter.28
  1476.7 38.4 reduce-scatter.20
  1518.0 29.2 reduce-scatter.24
  1549.6 28.5 reduce-scatter.26
  1581.6 50.3 all-reduce.31
where the time goes:
time: 1660 us; the launch traced here: 1650 us
  waiting for transfers between devices  799 us (48%)
  matrix products  277 us (17%)
  blocking collectives  219 us (13%)
  local copies, waits for them, and re-layouts  194 us (12%)
  other arithmetic  129 us (8%)
  between operations  16.8 us (1%)
    psum x2, waiting for transfers between devices, one_batch(): lax.psum(jnp.einsum('htd,hdn->tn', mix_in, out_heads, preferred_element_t...  122 us
    all_gather x2, waiting for transfers between devices, one_batch(): lax.all_gather(gate_up, 'shard', axis=1, tiled=True)  117 us
    while x22, waiting for transfers between devices  107 us
    psum x2, waiting for transfers between devices, one_batch(): lax.psum(jnp.dot(down_in, down_full, preferred_element_type=f32).astype(j...  90.7 us
    psum x2, waiting for transfers between devices, one_batch(): d_second = lax.psum(d_second_part, 'tp')  84.6 us
    unnamed x12, waiting for transfers between devices  83.4 us
    dynamic_update_slice x4, local copies, waits for them, and re-layouts, one_batch(): lax.dynamic_update_index_in_dim(carried[1], d_tokens, batch_idx, 0)  81.3 us
    unnamed x53, local copies, waits for them, and re-layouts  65.4 us
  transfers between devices with their start and end apart: 27, of which 22 were waited for; matrix products, arithmetic and copies ran while one was open for 17% of the time, Pallas kernels for 0%

commit v1 on v0

--- a/solution.py
+++ b/solution.py
@@ -1,11 +1,14 @@
+import functools
 import math
 
 import jax
 import jax.numpy as jnp
 from jax import lax
+from jax.experimental import pallas as pl
+from jax.experimental.pallas import tpu as pltpu
 from jax.sharding import PartitionSpec as P
 
-FF = 2730
+SHARD, CTX, TP = "shard", "ctx", "tp"
 
 
 EPS = 1e-06
@@ -57,7 +60,7 @@
     return jnp.sum(values.astype(jnp.float32), axis=0)
 
 
-def per_device(
+def general_plan(
     tokens,
     cotangent,
     valid_tokens,
@@ -79,20 +82,21 @@
     local_heads = head_biases.shape[1]
     head_size = local_dim // local_heads
     local_hidden = hidden_gain.shape[0]
+    FF = local_hidden * lax.axis_size(TP)
     score_scale = 1.0 / math.sqrt(head_size)
     f32 = jnp.float32
     bf16 = jnp.bfloat16
 
     def one_batch(batch_idx, carried):
         gathered = (
-            lax.all_gather(qkv_weight, "shard", axis=1, tiled=True),
-            lax.all_gather(head_biases, "shard", axis=2, tiled=True),
-            lax.all_gather(head_gain, "shard", axis=1, tiled=True),
-            lax.all_gather(out_weight, "shard", axis=1, tiled=True),
-            lax.all_gather(norm_gains, "shard", axis=1, tiled=True),
-            lax.all_gather(width_biases, "shard", axis=1, tiled=True),
-            lax.all_gather(gate_up, "shard", axis=1, tiled=True),
-            lax.all_gather(down_weight, "shard", axis=1, tiled=True),
+            lax.all_gather(qkv_weight, SHARD, axis=1, tiled=True),
+            lax.all_gather(head_biases, SHARD, axis=2, tiled=True),
+            lax.all_gather(head_gain, SHARD, axis=1, tiled=True),
+            lax.all_gather(out_weight, SHARD, axis=1, tiled=True),
+            lax.all_gather(norm_gains, SHARD, axis=1, tiled=True),
+            lax.all_gather(width_biases, SHARD, axis=1, tiled=True),
+            lax.all_gather(gate_up, SHARD, axis=1, tiled=True),
+            lax.all_gather(down_weight, SHARD, axis=1, tiled=True),
         )
         qkv_full, head_bias, head_scale, out_full, norm_scale, width_bias, gate_full, down_full = (
             gathered
@@ -123,8 +127,8 @@
         queries = rotate(query_pre, angles).astype(bf16)
         key_local = rotate(key_pre, angles).astype(bf16)
         key_heads, value_heads = (
-            lax.all_gather(key_local, "ctx", axis=1, tiled=True),
-            lax.all_gather(value_local, "ctx", axis=1, tiled=True),
+            lax.all_gather(key_local, CTX, axis=1, tiled=True),
+            lax.all_gather(value_local, CTX, axis=1, tiled=True),
         )
 
         def score_block():
@@ -144,14 +148,14 @@
                 jnp.sum(mixed, axis=(0, 2), keepdims=True),
                 jnp.sum(mixed * mixed, axis=(0, 2), keepdims=True),
             ),
-            "tp",
+            TP,
         )
         mix_mean = mix_sums[0] / width
         spread_mix = lax.rsqrt(mix_sums[1] / width - mix_mean * mix_mean + EPS)
         mix_hat = (mixed - mix_mean) * spread_mix
         mix_in = (mix_hat * head_scale_f + head_bias_f[2][:, None, :]).astype(bf16)
         branch = lax.psum(
-            jnp.einsum("htd,hdn->tn", mix_in, out_heads, preferred_element_type=f32), "tp"
+            jnp.einsum("htd,hdn->tn", mix_in, out_heads, preferred_element_type=f32), TP
         )
         resid = token_rows + (branch + width_bias[2])
         normed_two, spread_two = standardize(resid)
@@ -166,14 +170,14 @@
                 jnp.sum(hidden, axis=-1, keepdims=True),
                 jnp.sum(hidden * hidden, axis=-1, keepdims=True),
             ),
-            "tp",
+            TP,
         )
         hidden_mean = hidden_sums[0] / FF
         spread_hid = lax.rsqrt(hidden_sums[1] / FF - hidden_mean * hidden_mean + EPS)
         hidden_hat = (hidden - hidden_mean) * spread_hid
         down_in = (hidden_hat * hidden_scale + hidden_bias[2]).astype(bf16)
         ffn_out = lax.psum(
-            jnp.dot(down_in, down_full, preferred_element_type=f32).astype(jnp.bfloat16), "tp"
+            jnp.dot(down_in, down_full, preferred_element_type=f32).astype(jnp.bfloat16), TP
         ).astype(jnp.float32)
         result = (resid + (ffn_out + width_bias[3])).astype(bf16)
         d_ffn_low = cot_rows.astype(bf16)
@@ -185,7 +189,7 @@
                 jnp.sum(grad_hid, axis=-1, keepdims=True),
                 jnp.sum(grad_hid * hidden_hat, axis=-1, keepdims=True),
             ),
-            "tp",
+            TP,
         )
         d_hidden = (grad_hid - hid_back[0] / FF - hidden_hat * (hid_back[1] / FF)) * spread_hid
         d_gate = (
@@ -197,7 +201,7 @@
         d_second_part = jnp.einsum(
             "tf,df->td", d_gate, gate_full[0], preferred_element_type=f32
         ) + jnp.einsum("tf,df->td", d_up, gate_full[1], preferred_element_type=f32)
-        d_second = lax.psum(d_second_part, "tp")
+        d_second = lax.psum(d_second_part, TP)
         d_resid = cot_rows + norm_back(d_second * norm_scale[1], normed_two, spread_two)
         d_branch_low = d_resid.astype(bf16)
         g_out = jnp.einsum("htd,tn->hdn", mix_in, d_branch_low, preferred_element_type=f32).reshape(
@@ -210,7 +214,7 @@
                 jnp.sum(grad_mix, axis=(0, 2), keepdims=True),
                 jnp.sum(grad_mix * mix_hat, axis=(0, 2), keepdims=True),
             ),
-            "tp",
+            TP,
         )
         d_mixed = (
             (grad_mix - mix_back[0] / width - mix_hat * (mix_back[1] / width)) * spread_mix
@@ -231,10 +235,10 @@
         d_value_all = jnp.einsum("hts,htd->hsd", soft_again, d_mixed, preferred_element_type=f32)
         d_key_heads, d_value_loc = (
             lax.psum_scatter(
-                d_key_all.astype(jnp.bfloat16), "ctx", scatter_dimension=1, tiled=True
+                d_key_all.astype(jnp.bfloat16), CTX, scatter_dimension=1, tiled=True
             ).astype(jnp.float32),
             lax.psum_scatter(
-                d_value_all.astype(jnp.bfloat16), "ctx", scatter_dimension=1, tiled=True
+                d_value_all.astype(jnp.bfloat16), CTX, scatter_dimension=1, tiled=True
             ).astype(jnp.float32),
         )
         d_query_low = unrotate(d_query, angles).astype(bf16)
@@ -267,7 +271,7 @@
             qkv_full[2].reshape(width, local_heads, head_size),
             preferred_element_type=f32,
         )
-        d_first = lax.psum(d_first_part.astype(jnp.bfloat16), "tp").astype(jnp.float32)
+        d_first = lax.psum(d_first_part.astype(jnp.bfloat16), TP).astype(jnp.float32)
         d_tokens = d_resid + norm_back(d_first * norm_scale[0], normed_one, spread_one)
         g_head_bias = jnp.stack(
             [
@@ -355,96 +359,1216 @@
         acc_gate,
         acc_down,
     )
-    hidden_done = lax.psum((acc_hidden_bias, acc_hidden_scale), ("shard", "ctx"))
+    hidden_done = lax.psum((acc_hidden_bias, acc_hidden_scale), (SHARD, CTX))
     return (
         out_all,
         grad_all,
         lax.psum_scatter(
-            lax.psum(sharded[0].astype(jnp.bfloat16), "ctx"),
-            "shard",
+            lax.psum(sharded[0].astype(jnp.bfloat16), CTX),
+            SHARD,
             scatter_dimension=1,
             tiled=True,
         ).astype(jnp.float32),
         lax.psum_scatter(
-            lax.psum(sharded[1].astype(jnp.bfloat16), "ctx"),
-            "shard",
+            lax.psum(sharded[1].astype(jnp.bfloat16), CTX),
+            SHARD,
             scatter_dimension=2,
             tiled=True,
         ).astype(jnp.float32),
         lax.psum_scatter(
-            lax.psum(sharded[2].astype(jnp.bfloat16), "ctx"),
-            "shard",
+            lax.psum(sharded[2].astype(jnp.bfloat16), CTX),
+            SHARD,
             scatter_dimension=1,
             tiled=True,
         ).astype(jnp.float32),
         lax.psum_scatter(
-            lax.psum(sharded[3].astype(jnp.bfloat16), "ctx"),
-            "shard",
+            lax.psum(sharded[3].astype(jnp.bfloat16), CTX),
+            SHARD,
             scatter_dimension=1,
             tiled=True,
         ).astype(jnp.float32),
         lax.psum_scatter(
-            lax.psum(sharded[4].astype(jnp.bfloat16), "ctx"),
-            "shard",
+            lax.psum(sharded[4].astype(jnp.bfloat16), CTX),
+            SHARD,
             scatter_dimension=1,
             tiled=True,
         ).astype(jnp.float32),
         lax.psum_scatter(
-            lax.psum(sharded[5].astype(jnp.bfloat16), "ctx"),
-            "shard",
+            lax.psum(sharded[5].astype(jnp.bfloat16), CTX),
+            SHARD,
             scatter_dimension=1,
             tiled=True,
         ).astype(jnp.float32),
         lax.psum_scatter(
-            lax.psum(sharded[6].astype(jnp.bfloat16), "ctx"),
-            "shard",
+            lax.psum(sharded[6].astype(jnp.bfloat16), CTX),
+            SHARD,
             scatter_dimension=1,
             tiled=True,
         ).astype(jnp.float32),
         hidden_done[0],
         hidden_done[1],
         lax.psum_scatter(
-            lax.psum(sharded[7].astype(jnp.bfloat16), "ctx"),
-            "shard",
+            lax.psum(sharded[7].astype(jnp.bfloat16), CTX),
+            SHARD,
             scatter_dimension=1,
             tiled=True,
         ).astype(jnp.float32),
     )
 
 
+MESH = pl.DeviceIdType.MESH
+LIMIT = 56 * 1024 * 1024
+ANY = pl.BlockSpec(memory_space=pl.ANY)
+IN_VMEM = pl.BlockSpec(memory_space=pltpu.VMEM)
+CORE, ACROSS, BESIDE, UP, DOWN, SWAP, FAR = range(7)
+ROW, COL = range(2)
+
+
+def place_of():
+    index = lax.axis_index(SHARD)
+    return (lax.div(index, 2), lax.rem(index, 2), lax.axis_index(CTX), lax.axis_index(TP))
+
+
+def when(condition, action):
+    if condition is None:
+        action()
+    else:
+        pl.when(condition)(action)
+
+
+def both(first, second):
+    return jnp.logical_and(first, second)
+
+
+def device(place, way):
+    z, k, x, y = place
+    return {
+        CORE: {SHARD: 2 * z + 1 - k},
+        ACROSS: {CTX: 1 - x},
+        BESIDE: {TP: 1 - y},
+        UP: {SHARD: 2 * z + 2 + k},
+        DOWN: {SHARD: 2 * z - 2 + k},
+        SWAP: {SHARD: 2 * z + 1 - k, CTX: 1 - x},
+        FAR: {SHARD: 2 * z + 1 - k, CTX: 1 - x, TP: 1 - y},
+    }[way]
+
+
+def greet(layers, place, diagonals):
+    z, k, x, y = place
+    barrier = pltpu.get_barrier_semaphore()
+
+    def hello(way):
+        pl.semaphore_signal(barrier, inc=1, device_id=device(place, way), device_id_type=MESH)
+
+    hello(CORE)
+    hello(ACROSS)
+    hello(BESIDE)
+    pl.when(z > 0)(lambda: hello(DOWN))
+    pl.when(z < layers - 1)(lambda: hello(UP))
+    count = 3 + jnp.where(z > 0, 1, 0) + jnp.where(z < layers - 1, 1, 0)
+    for way in diagonals:
+        pl.when(k != x)(lambda way=way: hello(way))
+        count = count + jnp.where(k != x, 1, 0)
+    pl.semaphore_wait(barrier, count)
+
+
+class Links:
+    def __init__(self, place, send_sem, recv_sem):
+        self.place, self.send_sem, self.recv_sem = place, send_sem, recv_sem
+        self.used = 0
+        self.sent = []
+
+    def take(self, count):
+        first = self.used
+        self.used += count
+        return first
+
+    def copy(self, way, at, source, target):
+        return pltpu.make_async_remote_copy(
+            src_ref=source,
+            dst_ref=target,
+            send_sem=self.send_sem.at[at],
+            recv_sem=self.recv_sem.at[at],
+            device_id=device(self.place, way),
+            device_id_type=MESH,
+        )
+
+    def send(self, condition, copy):
+        when(condition, copy.start)
+        self.sent.append((condition, copy))
+
+    def finish(self):
+        for condition, copy in self.sent:
+            when(condition, copy.wait_send)
+
+
+def piece_view(kind, rows, cols, ref, y, s, first, size):
+    if kind == ROW:
+        at_row, at_col = s * rows + first, y * cols
+    else:
+        at_row, at_col = y * rows + first, s * cols
+    at_row, at_col = pl.multiple_of(at_row, 16), pl.multiple_of(at_col, 128)
+    return ref.at[pl.ds(at_row, size), pl.ds(at_col, cols)]
+
+
+def cut_rows(ref, first, size):
+    return ref.at[pl.ds(pl.multiple_of(first, 16), size), :]
+
+
+class Gather:
+    def __init__(self, layers, links, kind, own, full, split, local_sem):
+        self.layers, self.links, self.kind, self.own, self.full = layers, links, kind, own, full
+        self.rows, self.cols = own.shape
+        self.split, self.half = split, split // 2
+        self.local_sem = local_sem
+        n = layers
+        self.z_a = links.take(2 * n)
+        self.z_b = links.take(2 * n)
+        self.x_a, self.x_b = links.take(n), links.take(n)
+        self.y_a, self.y_b = links.take(n), links.take(1)
+        self.core_a, self.core_b = links.take(2 * n), links.take(2 * n)
+
+    @staticmethod
+    def sem_count(layers):
+        return 11 * layers + 1
+
+    def copy(self, way, at, y, z, first, size, from_own=False, other_core=False):
+        k = self.links.place[1]
+        s = 2 * z + (1 - k if other_core else k)
+        there = piece_view(self.kind, self.rows, self.cols, self.full, y, s, first, size)
+        here = cut_rows(self.own, first, size) if from_own else there
+        return self.links.copy(way, at, here, there)
+
+    def half_a(self, way, at, y, z, which, from_own=False):
+        return self.copy(way, at, y, z, which * self.half, self.half, from_own)
+
+    def part_a(self, way, at, y, z, from_own=False, other_core=False):
+        return self.copy(way, at, y, z, 0, self.split, from_own, other_core)
+
+    def part_b(self, way, at, y, z, from_own=False, other_core=False):
+        return self.copy(
+            way, at, y, z, self.split, self.rows - self.split, from_own, other_core
+        )
+
+    def z_at(self, base, way, z):
+        return base + (0 if way == UP else self.layers) + z
+
+    def core_at(self, base, y, z):
+        return base + 2 * z + y
+
+    def begin(self):
+        z, k, x, y = self.links.place
+        send = self.links.send
+        low, high = z > 0, z < self.layers - 1
+        own_view = piece_view(
+            self.kind, self.rows, self.cols, self.full, y, 2 * z + k, 0, self.rows
+        )
+        self.local = pltpu.make_async_copy(self.own, own_view, self.local_sem)
+        if self.split < self.rows:
+            send(None, self.part_b(BESIDE, self.y_b, y, z, True))
+            same = x == y
+            send(both(same, high), self.part_b(UP, self.z_at(self.z_b, UP, z), y, z, True))
+            send(both(same, low), self.part_b(DOWN, self.z_at(self.z_b, DOWN, z), y, z, True))
+        if self.split:
+            send(high, self.half_a(UP, self.z_at(self.z_a, UP, z), y, z, x, True))
+            send(low, self.half_a(DOWN, self.z_at(self.z_a, DOWN, z), y, z, x, True))
+            send(None, self.part_a(BESIDE, self.y_a + z, y, z, True))
+            send(None, self.part_a(CORE, self.core_at(self.core_a, y, z), y, z, True))
+        if self.split < self.rows:
+            send(None, self.part_b(CORE, self.core_at(self.core_b, y, z), y, z, True))
+        self.local.start()
+
+    def cross_y(self):
+        if self.split == self.rows:
+            return
+        z, k, x, y = self.links.place
+        send = self.links.send
+        self.part_b(BESIDE, self.y_b, 1 - y, z).wait_recv()
+        other = x != y
+        low, high = z > 0, z < self.layers - 1
+        send(both(other, high), self.part_b(UP, self.z_at(self.z_b, UP, z), 1 - y, z))
+        send(both(other, low), self.part_b(DOWN, self.z_at(self.z_b, DOWN, z), 1 - y, z))
+        send(None, self.part_b(CORE, self.core_at(self.core_b, 1 - y, z), 1 - y, z))
+
+    def steps(self, step):
+        z = self.links.place[0]
+        below, above = z - 1 - step, z + 1 + step
+        return (
+            (UP, below, below >= 0, z < self.layers - 1),
+            (DOWN, above, above <= self.layers - 1, z > 0),
+        )
+
+    def along_z(self, step):
+        z, k, x, y = self.links.place
+        send = self.links.send
+        for way, origin, there, further in self.steps(step):
+            if self.split < self.rows:
+                came = self.part_b(way, self.z_at(self.z_b, way, origin), x, origin)
+                when(there, came.wait_recv)
+                send(both(there, further), came)
+                send(there, self.part_b(ACROSS, self.x_b + origin, x, origin))
+                send(there, self.part_b(CORE, self.core_at(self.core_b, x, origin), x, origin))
+            if self.split:
+                came = self.half_a(way, self.z_at(self.z_a, way, origin), y, origin, x)
+                when(there, came.wait_recv)
+                send(both(there, further), came)
+                send(there, self.half_a(ACROSS, self.x_a + origin, y, origin, x))
+
+    def along_x(self, step):
+        z, k, x, y = self.links.place
+        send = self.links.send
+        for way, origin, there, further in self.steps(step):
+            if self.split:
+                when(there, self.half_a(ACROSS, self.x_a + origin, y, origin, 1 - x).wait_recv)
+                send(there, self.part_a(BESIDE, self.y_a + origin, y, origin))
+                send(there, self.part_a(CORE, self.core_at(self.core_a, y, origin), y, origin))
+            if self.split < self.rows:
+                when(there, self.part_b(ACROSS, self.x_b + origin, 1 - x, origin).wait_recv)
+                at = self.core_at(self.core_b, 1 - x, origin)
+                send(there, self.part_b(CORE, at, 1 - x, origin))
+
+    def along_y(self, step):
+        if not self.split:
+            return
+        z, k, x, y = self.links.place
+        send = self.links.send
+        todo = ((None, z, None, None),) if step < 0 else self.steps(step)
+        for way, origin, there, further in todo:
+            when(there, self.part_a(BESIDE, self.y_a + origin, 1 - y, origin).wait_recv)
+            at = self.core_at(self.core_a, 1 - y, origin)
+            send(there, self.part_a(CORE, at, 1 - y, origin))
+
+    def stages(self):
+        found = [[self.begin], [self.cross_y]]
+        for step in range(self.layers + 1):
+            now = []
+            if step < self.layers - 1:
+                now.append(functools.partial(self.along_z, step))
+            if step == 0:
+                now.append(functools.partial(self.along_y, -1))
+            if 0 <= step - 1 < self.layers - 1:
+                now.append(functools.partial(self.along_x, step - 1))
+            if 0 <= step - 2 < self.layers - 1:
+                now.append(functools.partial(self.along_y, step - 2))
+            found.append(now)
+        return found
+
+    def arrived(self):
+        self.local.wait()
+        for layer in range(self.layers):
+            for y in range(2):
+                if self.split:
+                    at = self.core_at(self.core_a, y, layer)
+                    self.part_a(CORE, at, y, layer, other_core=True).wait_recv()
+                if self.split < self.rows:
+                    at = self.core_at(self.core_b, y, layer)
+                    self.part_b(CORE, at, y, layer, other_core=True).wait_recv()
+
+
+def ticks_of(jobs, lead):
+    plans = [job.stages() for job in jobs]
+    ticks = [[] for _ in range(len(jobs) + max([len(plan) for plan in plans]))]
+    for number, plan in enumerate(plans):
+        for stage, actions in enumerate(plan):
+            at = max(0, number - lead) if stage == 0 else number + stage
+            ticks[at] += actions
+    return [tick for tick in ticks if tick]
+
+
+class Swap:
+    def __init__(self, links, source, target, local_sem):
+        z, k, x, y = links.place
+        self.same, self.other = k == x, k != x
+        self.here = pltpu.make_async_copy(source, target, local_sem)
+        self.there = links.copy(SWAP, links.take(1), source, target)
+
+    def begin(self):
+        pl.when(self.same)(self.here.start)
+        pl.when(self.other)(self.there.start)
+
+    def arrived(self):
+        pl.when(self.same)(self.here.wait)
+        pl.when(self.other)(self.there.wait)
+
+
+class Cross:
+    def __init__(self, links, source, target, local_sem):
+        y = links.place[3]
+        at = links.take(1)
+        self.here = pltpu.make_async_copy(source, target.at[y], local_sem)
+        self.out = links.copy(BESIDE, at, source, target.at[y])
+        self.back = links.copy(BESIDE, at, source, target.at[1 - y])
+
+    def begin(self):
+        self.here.start()
+        self.out.start()
+
+    def arrived(self):
+        self.here.wait()
+        self.out.wait_send()
+        self.back.wait_recv()
+
+
+class Spread:
+    def __init__(self, links, block, both_images, local_sem):
+        z, k, x, y = links.place
+        self.same, self.other = k == x, k != x
+        here, first, second = links.take(1), links.take(1), 0
+        target = both_images.at[y]
+        self.keep = pltpu.make_async_copy(block, target, local_sem)
+        self.beside = links.copy(BESIDE, here, block, target)
+        self.swap = links.copy(SWAP, first, block, target)
+        self.far = links.copy(FAR, here, block, target)
+        self.came = links.copy(BESIDE, here, block, both_images.at[1 - y])
+
+    def begin(self):
+        def same():
+            self.keep.start()
+            self.beside.start()
+
+        def other():
+            self.swap.start()
+            self.far.start()
+
+        pl.when(self.same)(same)
+        pl.when(self.other)(other)
+
+    def arrived(self):
+        def same():
+            self.keep.wait()
+            self.beside.wait_send()
+
+        def other():
+            self.swap.wait()
+            self.far.wait_send()
+
+        pl.when(self.same)(same)
+        pl.when(self.other)(other)
+        self.came.wait_recv()
+
+
+def gather_kernel(layers, jobs, swaps, crosses, mats, *refs):
+    own, refs = refs[:mats], refs[mats:]
+    swap_in, refs = refs[:swaps], refs[swaps:]
+    cross_in, refs = refs[:crosses], refs[crosses:]
+    full, refs = refs[:mats], refs[mats:]
+    swap_out, refs = refs[:swaps], refs[swaps:]
+    cross_out, refs = refs[:crosses], refs[crosses:]
+    send_sem, recv_sem, local_sem = refs
+    place = place_of()
+    greet(layers, place, (SWAP,) if swaps else ())
+    links = Links(place, send_sem, recv_sem)
+    y = place[3]
+    extras = []
+    for source, target in zip(swap_in, swap_out):
+        if len(source.shape) > len(target.shape):
+            source = source.at[y]
+        extras.append(Swap(links, source, target, local_sem.at[len(extras)]))
+    for source, target in zip(cross_in, cross_out):
+        extras.append(Cross(links, source, target, local_sem.at[len(extras)]))
+    for extra in extras:
+        extra.begin()
+    todo = []
+    for mat, lead, kind, split in jobs:
+        piece, whole = own[mat], full[mat]
+        if lead is not None:
+            piece, whole = piece.at[lead], whole.at[lead]
+        at = local_sem.at[len(extras) + len(todo)]
+        todo.append(Gather(layers, links, kind, piece, whole, split, at))
+    for tick in ticks_of(todo, 1):
+        for action in tick:
+            action()
+    for job in todo + extras:
+        job.arrived()
+    links.finish()
+
+
+def full_shape(layers, kind, piece):
+    if kind == ROW:
+        return piece[:-2] + (piece[-2] * layers * 2, piece[-1] * 2)
+    return (piece[-2] * 2, piece[-1] * layers * 2)
+
+
+def gather(layers, number, jobs, own, swap_in=(), cross_in=()):
+    kinds = {job[0]: job[2] for job in jobs}
+    shapes = [
+        jax.ShapeDtypeStruct(full_shape(layers, kinds[i], piece.shape), piece.dtype)
+        for i, piece in enumerate(own)
+    ]
+    for item in swap_in:
+        big = item.dtype == jnp.bfloat16
+        shapes.append(jax.ShapeDtypeStruct(item.shape[1:] if big else item.shape, item.dtype))
+    for item in cross_in:
+        shapes.append(jax.ShapeDtypeStruct((2,) + item.shape, item.dtype))
+    extra = len(swap_in) + len(cross_in)
+    sems = len(jobs) * Gather.sem_count(layers) + extra
+    given = list(own) + list(swap_in) + list(cross_in)
+    return pl.pallas_call(
+        functools.partial(gather_kernel, layers, jobs, len(swap_in), len(cross_in), len(own)),
+        out_shape=shapes,
+        in_specs=[ANY] * len(given),
+        out_specs=[ANY] * len(shapes),
+        scratch_shapes=[
+            pltpu.SemaphoreType.DMA((sems,)),
+            pltpu.SemaphoreType.DMA((sems,)),
+            pltpu.SemaphoreType.DMA((len(jobs) + extra,)),
+        ],
+        compiler_params=pltpu.CompilerParams(collective_id=number, has_side_effects=True),
+    )(*given)
+
+
+def by_chunks(shape, body):
+    rows, cols = shape
+    chunk = 16
+    while rows % (2 * chunk) == 0 and 2 * chunk * cols <= 16384:
+        chunk *= 2
+
+    def step(i, nothing):
+        body((pl.ds(pl.multiple_of(i * chunk, 16), chunk), slice(None)))
+        return nothing
+
+    lax.fori_loop(0, rows // chunk, step, 0)
+
+
+def add_into(target, term):
+    def body(where):
+        total = target[where].astype(jnp.float32) + term[where].astype(jnp.float32)
+        target[where] = total.astype(target.dtype)
+
+    by_chunks(target.shape, body)
+
+
+def store_sum(out, *terms):
+    def body(where):
+        total = terms[0][where].astype(jnp.float32)
+        for term in terms[1:]:
+            total = total + term[where].astype(jnp.float32)
+        out[where] = total
+
+    by_chunks(out.shape, body)
+
+
+class Reduce:
+    def __init__(self, layers, links, kind, grad, out, split, scratch, local_sem, local_base):
+        self.layers, self.links, self.kind, self.grad, self.out = layers, links, kind, grad, out
+        self.mine, self.core_in, self.y_in, self.x_in, self.up_in, self.down_in, self.last = scratch
+        self.rows, self.cols = self.mine.shape[-2:]
+        self.split = split
+        self.local_sem, self.local_base = local_sem, local_base
+        n = layers
+        self.core = links.take(2 * n)
+        self.y_a, self.x_b = links.take(n), links.take(n)
+        self.z_a, self.z_b = links.take(2 * n), links.take(2 * n)
+        self.end_a, self.end_b, self.end_c = links.take(1), links.take(1), links.take(1)
+        self.order = []
+        low, high = 0, layers - 1
+        while low <= high:
+            self.order.append(high)
+            if low < high:
+                self.order.append(low)
+            low, high = low + 1, high - 1
+
+    @staticmethod
+    def sem_count(layers):
+        return 8 * layers + 3
+
+    def part_a(self, ref):
+        return cut_rows(ref, 0, self.split)
+
+    def part_b(self, ref):
+        return cut_rows(ref, self.split, self.rows - self.split)
+
+    def grad_piece(self, y, s):
+        return piece_view(self.kind, self.rows, self.cols, self.grad, y, s, 0, self.rows)
+
+    def local(self, y, layer):
+        k = self.links.place[1]
+        return pltpu.make_async_copy(
+            self.grad_piece(y, 2 * layer + k),
+            self.mine.at[y, layer],
+            self.local_sem.at[self.local_base + 2 * layer + y],
+        )
+
+    def to_core(self, y, layer):
+        k = self.links.place[1]
+        return self.links.copy(
+            CORE,
+            self.core + 2 * layer + y,
+            self.grad_piece(y, 2 * layer + 1 - k),
+            self.core_in.at[y, layer],
+        )
+
+    def begin(self):
+        for layer in self.order:
+            for y in range(2):
+                self.links.send(None, self.to_core(y, layer))
+                self.local(y, layer).start()
+
+    def to_y(self, layer):
+        y = self.links.place[3]
+        source = self.part_a(self.mine.at[1 - y, layer])
+        return self.links.copy(BESIDE, self.y_a + layer, source, self.y_in.at[layer])
+
+    def to_x(self, layer):
+        x = self.links.place[2]
+        source = self.part_b(self.mine.at[1 - x, layer])
+        return self.links.copy(ACROSS, self.x_b + layer, source, self.x_in.at[layer])
+
+    def chip_sum(self):
+        for layer in self.order:
+            for side in range(2):
+                self.local(side, layer).wait()
+                self.to_core(side, layer).wait_recv()
+                add_into(self.mine.at[side, layer], self.core_in.at[side, layer])
+            self.links.send(None, self.to_y(layer))
+            self.links.send(None, self.to_x(layer))
+
+    def plane_sum(self):
+        z, k, x, y = self.links.place
+        for layer in self.order:
+            self.to_y(layer).wait_recv()
+            add_into(self.part_a(self.mine.at[y, layer]), self.y_in.at[layer])
+            self.to_x(layer).wait_recv()
+            add_into(self.part_b(self.mine.at[x, layer]), self.x_in.at[layer])
+
+    def chain(self, way, layer):
+        z, k, x, y = self.links.place
+        inbox = self.up_in if way == UP else self.down_in
+        add = 0 if way == UP else self.layers
+        found = []
+        for base, part, side in ((self.z_a, self.part_a, y), (self.z_b, self.part_b, x)):
+            total, box = part(self.mine.at[side, layer]), part(inbox.at[layer])
+            found.append((total, box, self.links.copy(way, base + add + layer, total, box)))
+        return found
+
+    def take(self, way, layer):
+        for total, box, copy in self.chain(way, layer):
+            copy.wait_recv()
+            add_into(total, box)
+
+    def along_z(self, depth):
+        z = self.links.place[0]
+        top = self.layers - 1
+        for way, here, goals in (
+            (UP, z == depth, range(top, depth, -1)),
+            (DOWN, z == top - depth, range(0, top - depth)),
+        ):
+            for layer in goals:
+                if depth:
+                    pl.when(here)(functools.partial(self.take, way, layer))
+                for total, box, copy in self.chain(way, layer):
+                    self.links.send(here, copy)
+
+    def ending(self):
+        z, k, x, y = self.links.place
+        pl.when(z > 0)(functools.partial(self.take, UP, z))
+        pl.when(z < self.layers - 1)(functools.partial(self.take, DOWN, z))
+        self.sum_a, self.sum_b = self.part_a(self.mine.at[y, z]), self.part_b(self.mine.at[x, z])
+        self.got_a, self.got_b = self.part_a(self.last.at[0]), self.part_b(self.last.at[0])
+        self.got_y = self.part_b(self.last.at[1])
+        self.x_end = self.links.copy(ACROSS, self.end_a, self.sum_a, self.got_a)
+        self.y_end = self.links.copy(BESIDE, self.end_b, self.sum_b, self.got_y)
+        self.x_last = self.links.copy(ACROSS, self.end_c, self.sum_b, self.got_b)
+        self.links.send(y != x, self.y_end)
+        self.links.send(None, self.x_end)
+
+    def owner(self):
+        z, k, x, y = self.links.place
+
+        def own():
+            self.y_end.wait_recv()
+            add_into(self.sum_b, self.got_y)
+
+        pl.when(y == x)(own)
+        self.links.send(y == x, self.x_last)
+        self.x_end.wait_recv()
+        store_sum(self.part_a(self.out), self.sum_a, self.got_a)
+
+    def write(self):
+        z, k, x, y = self.links.place
+        out_b = self.part_b(self.out)
+
+        def received():
+            self.x_last.wait_recv()
+            store_sum(out_b, self.got_b)
+
+        pl.when(y != x)(received)
+        pl.when(y == x)(lambda: store_sum(out_b, self.sum_b))
+
+    def stages(self):
+        chains = [[functools.partial(self.along_z, depth)] for depth in range(self.layers - 1)]
+        return [
+            [self.begin], [self.chip_sum], [self.plane_sum], *chains,
+            [self.ending], [self.owner], [self.write],
+        ]
+
+
+class Total:
+    def __init__(self, layers, links, given, out, boxes, layer_boxes):
+        self.layers, self.links, self.given, self.out = layers, links, given, out
+        self.boxes, self.layer_boxes = boxes, layer_boxes
+        self.pair = [links.take(1) for _ in range(3)]
+        self.z_up, self.z_down = links.take(layers), links.take(layers)
+
+    @staticmethod
+    def sem_count(layers):
+        return 3 + 2 * layers
+
+    def exchange(self, number):
+        way = (CORE, ACROSS, BESIDE)[number]
+        source = self.given if number == 0 else self.boxes.at[2 + number]
+        return self.links.copy(way, self.pair[number], source, self.boxes.at[number])
+
+    def begin(self):
+        self.links.send(None, self.exchange(0))
+
+    def join(self, number):
+        z = self.links.place[0]
+        self.exchange(number).wait_recv()
+        mine = self.given if number == 0 else self.boxes.at[2 + number]
+        result = self.layer_boxes.at[z] if number == 2 else self.boxes.at[3 + number]
+        store_sum(result, mine, self.boxes.at[number])
+        if number < 2:
+            self.links.send(None, self.exchange(number + 1))
+        else:
+            self.links.send(z < self.layers - 1, self.pass_on(UP, z))
+            self.links.send(z > 0, self.pass_on(DOWN, z))
+
+    def pass_on(self, way, layer):
+        box = self.layer_boxes.at[layer]
+        return self.links.copy(way, (self.z_up if way == UP else self.z_down) + layer, box, box)
+
+    def along_z(self, step):
+        z = self.links.place[0]
+        top = self.layers - 1
+        below, above = z - 1 - step, z + 1 + step
+        for way, origin, there, further in (
+            (UP, below, below >= 0, z < top),
+            (DOWN, above, above <= top, z > 0),
+        ):
+            copy = self.pass_on(way, origin)
+            when(there, copy.wait_recv)
+            self.links.send(both(there, further), copy)
+
+    def write(self):
+        store_sum(self.out, *[self.layer_boxes.at[layer] for layer in range(self.layers)])
+
+    def stages(self):
+        joins = [[functools.partial(self.join, number)] for number in range(3)]
+        moves = [[functools.partial(self.along_z, step)] for step in range(self.layers - 1)]
+        return [[self.begin], *joins, *moves, [self.write]]
+
+
+def reduce_kernel(layers, jobs, mats, blocks, *refs):
+    grads, refs = refs[:mats], refs[mats:]
+    total_in, refs = refs[0], refs[1:]
+    block_in, refs = refs[:blocks], refs[blocks:]
+    outs, refs = refs[:mats], refs[mats:]
+    total_out, refs = refs[0], refs[1:]
+    block_out, refs = refs[:blocks], refs[blocks:]
+    scratch = refs[: 7 * len(jobs)]
+    boxes, layer_boxes, send_sem, recv_sem, local_sem = refs[7 * len(jobs) :]
+    place = place_of()
+    greet(layers, place, (SWAP, FAR))
+    links = Links(place, send_sem, recv_sem)
+    todo = []
+    for number, (mat, lead, kind, split) in enumerate(jobs):
+        grad, out = grads[mat], outs[mat]
+        if lead is not None:
+            grad, out = grad.at[lead], out.at[lead]
+        own = scratch[7 * number : 7 * number + 7]
+        at = number * 2 * layers
+        todo.append(Reduce(layers, links, kind, grad, out, split, own, local_sem, at))
+    todo.insert(1, Total(layers, links, total_in, total_out, boxes, layer_boxes))
+    extras = [
+        Spread(links, source, target, local_sem.at[len(jobs) * 2 * layers + i])
+        for i, (source, target) in enumerate(zip(block_in, block_out))
+    ]
+    for number, tick in enumerate(ticks_of(todo, 1)):
+        for action in tick:
+            action()
+        if number == 2:
+            for extra in extras:
+                extra.begin()
+    for extra in extras:
+        extra.arrived()
+    links.finish()
+
+
+def piece_shape(layers, kind, full):
+    if kind == ROW:
+        return full[:-2] + (full[-2] // (2 * layers), full[-1] // 2)
+    return (full[-2] // 2, full[-1] // (2 * layers))
+
+
+def reduce_grads(layers, number, jobs, grads, total, blocks):
+    kinds = {job[0]: job[2] for job in jobs}
+    pieces = [piece_shape(layers, kinds[i], g.shape) for i, g in enumerate(grads)]
+    scratch = []
+    for mat, lead, kind, split in jobs:
+        rows, cols = pieces[mat][-2:]
+        for lead_shape, here in (
+            ((2, layers), rows), ((2, layers), rows), ((layers,), split), ((layers,), rows - split),
+            ((layers,), rows), ((layers,), rows), ((2,), rows),
+        ):
+            scratch.append(pltpu.VMEM(lead_shape + (here, cols), jnp.bfloat16))
+    sems = len(jobs) * Reduce.sem_count(layers) + Total.sem_count(layers) + 2 * len(blocks)
+    images = [jax.ShapeDtypeStruct((2,) + block.shape, block.dtype) for block in blocks]
+    return pl.pallas_call(
+        functools.partial(reduce_kernel, layers, jobs, len(grads), len(blocks)),
+        out_shape=[jax.ShapeDtypeStruct(piece, jnp.float32) for piece in pieces]
+        + [jax.ShapeDtypeStruct(total.shape, total.dtype)]
+        + images,
+        in_specs=[ANY] * len(grads) + [IN_VMEM] + [ANY] * len(blocks),
+        out_specs=[IN_VMEM] * len(pieces) + [IN_VMEM] + [ANY] * len(blocks),
+        scratch_shapes=scratch
+        + [
+            pltpu.VMEM((5,) + total.shape, jnp.float32),
+            pltpu.VMEM((layers,) + total.shape, jnp.float32),
+            pltpu.SemaphoreType.DMA((sems,)),
+            pltpu.SemaphoreType.DMA((sems,)),
+            pltpu.SemaphoreType.DMA((len(jobs) * 2 * layers + len(blocks),)),
+        ],
+        compiler_params=pltpu.CompilerParams(
+            collective_id=number, has_side_effects=True, vmem_limit_bytes=LIMIT
+        ),
+    )(*grads, total, *blocks)
+
+
+def pair_lanes(shape, head_size):
+    lane = lax.broadcasted_iota(jnp.int32, shape, len(shape) - 1)
+    return lane < head_size
+
+
+def dot_last(left, right):
+    return lax.dot_general(left, right, (((1,), (1,)), ((), ())), preferred_element_type=jnp.float32)
+
+
+def dot_first(left, right):
+    return lax.dot_general(left, right, (((0,), (0,)), ((), ())), preferred_element_type=jnp.float32)
+
+
+def dot(left, right):
+    return lax.dot_general(left, right, (((1,), (0,)), ((), ())), preferred_element_type=jnp.float32)
+
+
+def only_head(values, head, head_size):
+    lane = lax.broadcasted_iota(jnp.int32, (1, values.shape[1]), 1)
+    keep = (lane < head_size) if head == 0 else (lane >= head_size)
+    return values * jnp.where(keep, 1.0, 0.0).astype(values.dtype)
+
+
+LOG2_E = 1.4426950408889634
+
+
+def mix_kernel(head_size, q_ref, k_ref, v_ref, bias_ref, o_ref, stat_ref):
+    scale = LOG2_E / math.sqrt(head_size)
+    q, k, v = q_ref[...], k_ref[...], v_ref[...]
+    bias = bias_ref[...]
+    parts = []
+    for head in range(2):
+        s = dot_last(only_head(q, head, head_size), k) * scale + bias
+        top = jnp.max(s, axis=1, keepdims=True)
+        e = jnp.exp2(s - top)
+        total = jnp.sum(e, axis=1, keepdims=True)
+        parts.append(dot(e.astype(jnp.bfloat16), v) * (1.0 / total))
+        level = jnp.broadcast_to(top + jnp.log2(total), (q.shape[0], 128))
+        stat_ref[0, head : head + 1, :] = jnp.transpose(level)[0:1, :]
+    o_ref[...] = jnp.where(pair_lanes(o_ref.shape, head_size), parts[0], parts[1])
+
+
+def mix_forward(q, k, v, bias, head_size):
+    rows, width = q.shape
+    keys = k.shape[0]
+    pairs = width // (2 * head_size)
+    lanes = 2 * head_size
+    return pl.pallas_call(
+        functools.partial(mix_kernel, head_size),
+        grid=(pairs,),
+        out_shape=[
+            jax.ShapeDtypeStruct((rows, width), jnp.float32),
+            jax.ShapeDtypeStruct((pairs, 2, rows), jnp.float32),
+        ],
+        in_specs=[
+            pl.BlockSpec((rows, lanes), lambda i: (0, i)),
+            pl.BlockSpec((keys, lanes), lambda i: (0, i)),
+            pl.BlockSpec((keys, lanes), lambda i: (0, i)),
+            pl.BlockSpec((1, keys), lambda i: (0, 0)),
+        ],
+        out_specs=[
+            pl.BlockSpec((rows, lanes), lambda i: (0, i)),
+            pl.BlockSpec((1, 2, rows), lambda i: (i, 0, 0)),
+        ],
+        compiler_params=pltpu.CompilerParams(vmem_limit_bytes=LIMIT),
+    )(q, k, v, bias)
+
+
+def mix_back_kernel(
+    head_size, q_ref, k_ref, v_ref, do_ref, stat_ref, dot_ref, bias_ref, dq_ref, dk_ref, dv_ref
+):
+    scale = 1.0 / math.sqrt(head_size)
+    q, k, v, do = q_ref[...], k_ref[...], v_ref[...], do_ref[...]
+    bias = bias_ref[...]
+    found = []
+    for head in range(2):
+        s = dot_last(k, only_head(q, head, head_size)) * (scale * LOG2_E) + bias
+        p = jnp.exp2(s - stat_ref[0, head : head + 1, :])
+        dp = dot_last(v, only_head(do, head, head_size))
+        ds = (p * (dp - dot_ref[0, head : head + 1, :])).astype(jnp.bfloat16)
+        dv = dot(p.astype(jnp.bfloat16), do)
+        dk = dot(ds, q) * scale
+        dq = dot_first(ds, k) * scale
+        found.append((dq, dk, dv))
+    for ref, first, second in zip((dq_ref, dk_ref, dv_ref), *found):
+        ref[...] = jnp.where(pair_lanes(ref.shape, head_size), first, second).astype(ref.dtype)
+
+
+def mix_backward(q, k, v, do, stats, row_dots, bias, head_size):
+    rows, width = q.shape
+    keys = k.shape[0]
+    pairs = width // (2 * head_size)
+    lanes = 2 * head_size
+    of_rows = pl.BlockSpec((rows, lanes), lambda i: (0, i))
+    of_keys = pl.BlockSpec((keys, lanes), lambda i: (0, i))
+    of_stats = pl.BlockSpec((1, 2, rows), lambda i: (i, 0, 0))
+    return pl.pallas_call(
+        functools.partial(mix_back_kernel, head_size),
+        grid=(pairs,),
+        out_shape=[
+            jax.ShapeDtypeStruct((rows, width), jnp.float32),
+            jax.ShapeDtypeStruct((keys, width), jnp.bfloat16),
+            jax.ShapeDtypeStruct((keys, width), jnp.bfloat16),
+        ],
+        in_specs=[
+            of_rows, of_keys, of_keys, of_rows, of_stats, of_stats,
+            pl.BlockSpec((keys, 1), lambda i: (0, 0)),
+        ],
+        out_specs=[of_rows, of_keys, of_keys],
+        compiler_params=pltpu.CompilerParams(vmem_limit_bytes=LIMIT),
+    )(q, k, v, do, stats, row_dots, bias)
+
+
+def turn_lanes(values, quarter):
+    width = values.shape[-1]
+    lane = lax.broadcasted_iota(jnp.int32, (1, width), 1)
+    even = lax.rem(lax.div(lane, quarter), 2) == 0
+    after = pltpu.roll(values, width - quarter, 1)
+    before = pltpu.roll(values, quarter, 1)
+    return jnp.where(even, -after, before)
+
+
+def project_kernel(quarter, tiles, x_ref, norm_ref, w_ref, bias_ref, cos_ref, sin_ref, out_ref, n_ref):
+    step = pl.program_id(0)
+
+    @pl.when(step == 0)
+    def _():
+        hat, spread = standardize(x_ref[...].astype(jnp.float32))
+        n_ref[...] = (hat * norm_ref[0:1, :] + norm_ref[1:2, :]).astype(jnp.bfloat16)
+
+    raw = dot(n_ref[...], w_ref[0]) + bias_ref[0]
+
+    @pl.when(step < 2 * tiles)
+    def _():
+        turned = turn_lanes(raw, quarter)
+        out_ref[0] = (raw * cos_ref[...] + turned * sin_ref[...]).astype(jnp.bfloat16)
+
+    @pl.when(step >= 2 * tiles)
+    def _():
+        out_ref[0] = raw.astype(jnp.bfloat16)
+
+
+def project(x, norm, weights, bias, cos, sin, head_size, tile=256):
+    rows, width = x.shape
+    tiles = width // tile
+    fixed = lambda i: (0, 0)
+    return pl.pallas_call(
+        functools.partial(project_kernel, head_size // 4, tiles),
+        grid=(3 * tiles,),
+        out_shape=[
+            jax.ShapeDtypeStruct((3, rows, width), jnp.bfloat16),
+            jax.ShapeDtypeStruct((rows, width), jnp.bfloat16),
+        ],
+        in_specs=[
+            pl.BlockSpec((rows, width), fixed),
+            pl.BlockSpec((2, width), fixed),
+            pl.BlockSpec((1, width, tile), lambda i: (i // tiles, 0, i % tiles)),
+            pl.BlockSpec((1, 1, tile), lambda i: (i // tiles, 0, i % tiles)),
+            pl.BlockSpec((rows, tile), fixed),
+            pl.BlockSpec((rows, tile), fixed),
+        ],
+        out_specs=[
+            pl.BlockSpec((1, rows, tile), lambda i: (i // tiles, 0, i % tiles)),
+            pl.BlockSpec((rows, width), fixed),
+        ],
+        compiler_params=pltpu.CompilerParams(vmem_limit_bytes=LIMIT),
+    )(x, norm, weights, bias, cos, sin)
+
+
+def pad_to(values, axis, size):
+    pads = [(0, 0)] * values.ndim
+    pads[axis] = (0, size - values.shape[axis])
+    return jnp.pad(values, pads)
+
+
+def round_up(size, step):
+    return (size + step - 1) // step * step
+
+
+def image_per_chip(
+    layers,
+    tokens,
+    cotangent,
+    valid_tokens,
+    places,
+    qkv_weight,
+    head_biases,
+    head_gain,
+    out_weight,
+    norm_gains,
+    width_biases,
+    gate_up,
+    hidden_biases,
+    hidden_gain,
+    down_weight,
+):
+    f32 = jnp.float32
+    bf16 = jnp.bfloat16
+    z, k, x, y = place_of()
+    s = 2 * z + k
+    shards = 2 * layers
+    width = tokens.shape[2]
+    rows = tokens.shape[1]
+    heads_here = head_gain.shape[0]
+    heads = 2 * heads_here
+    dims_here = head_gain.shape[1]
+    head_size = dims_here * shards
+    real_here = hidden_gain.shape[0]
+    hidden_here = round_up(real_here, 128)
+    real = 2 * real_here
+    hidden_size = 2 * hidden_here
+    score_scale = 1.0 / math.sqrt(head_size)
+
+    heads_flat = jnp.concatenate([head_biases, head_gain[None]], axis=0).reshape(-1, 128)
+    head_rows = heads_flat.shape[0]
+    vectors = jnp.concatenate([norm_gains, width_biases, heads_flat], axis=0)
+    vectors = pad_to(vectors, 0, 16)
+    hidden_vectors = jnp.concatenate([hidden_biases, hidden_gain[None]], axis=0)
+    hidden_vectors = pad_to(pad_to(hidden_vectors, 1, hidden_here), 0, 16)
+    gate_pad = pad_to(gate_up, 2, hidden_here)
+    down_pad = pad_to(down_weight, 0, hidden_here)
+
+    jobs = (
+        (0, 0, ROW, 64), (0, 1, ROW, 64), (0, 2, ROW, 64), (1, None, COL, 0),
+        (2, None, COL, 256), (3, 0, ROW, 64), (3, 1, ROW, 64), (4, None, COL, hidden_here // 2),
+    )
+    (
+        qkv_full, vector_full, out_full, gate_full, down_full,
+        token_block, cot_block, valid_both, place_both, hidden_full,
+    ) = gather(
+        layers, 0, jobs, (qkv_weight, vectors, out_weight, gate_pad, down_pad),
+        (tokens, cotangent, valid_tokens, places), (hidden_vectors,),
+    )
+    norm_scale = vector_full[0:2].astype(f32)
+    width_bias = vector_full[2:6].astype(f32)
+    head_part = jnp.stack([vector_full[6 : 6 + head_rows], vector_full[22 : 22 + head_rows]])
+    head_part = head_part.reshape(2, head_rows, shards, 128).transpose(0, 2, 1, 3)
+    head_part = head_part.reshape(2, shards, 4, heads_here, dims_here).transpose(2, 0, 3, 1, 4)
+    head_part = head_part.reshape(4, heads * head_size).astype(f32)
+    hidden_part = jnp.concatenate([hidden_full[0, :4], hidden_full[1, :4]], axis=1).astype(f32)
+
+    padded = round_up(rows, 16)
+    token_block = pad_to(token_block, 0, padded)
+    cot_block = pad_to(cot_block, 0, padded)
+    token_rows = token_block.astype(f32)
+    cot_rows = cot_block.astype(f32)
+    valid_row = lax.dynamic_index_in_dim(valid_both, y, 0, keepdims=False)
+    row_ids = pad_to(lax.dynamic_index_in_dim(place_both[0], y, 0, keepdims=False), 0, padded)
+    col_ids = pad_to(lax.dynamic_index_in_dim(place_both[1], y, 0, keepdims=False), 0, padded)
+    key_bias = jnp.where(pad_to(valid_row.reshape(2, rows), 1, padded) > 0, 0.0, -1e30)
+    key_bias = key_bias.astype(f32).reshape(1, 2 * padded)
+    angles = angle_table(row_ids, col_ids, head_size)
+    tile = 512
+    cos, sin = [jnp.tile(turn(angles), (1, tile // head_size)) for turn in (jnp.cos, jnp.sin)]
+    norm_one = jnp.stack([norm_scale[0], width_bias[0]])
+    qkv_bias = jnp.stack([head_part[0], jnp.zeros_like(head_part[0]), head_part[1]])[:, None]
+    qkv, first_in = project(token_block, norm_one, qkv_full, qkv_bias, cos, sin, head_size, tile)
+    pairs = [(i, i ^ 1) for i in range(shards)]
+    own = qkv[1:]
+    other = lax.ppermute(own, SHARD, pairs)
+    halves = jnp.stack([jnp.where(k == 0, own, other), jnp.where(k == 0, other, own)], axis=1)
+    keys = halves[0].reshape(2 * padded, width)
+    values = halves[1].reshape(2 * padded, width)
+    mixed, stats = mix_forward(qkv[0], keys, values, key_bias, head_size)
+    mix_hat, spread_mix = standardize(mixed)
+    mix_in = (mix_hat * head_part[3] + head_part[2]).astype(bf16)
+    branch = jnp.dot(mix_in, out_full, preferred_element_type=f32)
+    resid = token_rows + (branch + width_bias[2])
+    normed_two, spread_two = standardize(resid)
+    second_in = (normed_two * norm_scale[1] + width_bias[1]).astype(bf16)
+    gate_pre = jnp.dot(second_in, gate_full[0], preferred_element_type=f32) + hidden_part[0]
+    up_pre = jnp.dot(second_in, gate_full[1], preferred_element_type=f32) + hidden_part[1]
+    sigmoid_gate = jax.nn.sigmoid(gate_pre)
+    silu_gate = gate_pre * sigmoid_gate
+    hidden = silu_gate * up_pre
+    hidden_mean = jnp.sum(hidden, axis=-1, keepdims=True) / real
+    centred = hidden - hidden_mean
+    extra = (hidden_size - real) * hidden_mean * hidden_mean
+    hidden_var = (jnp.sum(centred * centred, axis=-1, keepdims=True) - extra) / real
+    spread_hid = lax.rsqrt(jnp.maximum(hidden_var, 0.0) + EPS)
+    hidden_hat = centred * spread_hid
+    down_in = (hidden_hat * hidden_part[3] + hidden_part[2]).astype(bf16)
+    ffn_out = jnp.dot(down_in, down_full, preferred_element_type=f32)
+    result = (resid + (ffn_out + width_bias[3])).astype(bf16)
+
+    g_down = jnp.einsum("tf,td->fd", down_in, cot_block, preferred_element_type=f32)
+    d_down_in = jnp.einsum("td,fd->tf", cot_block, down_full, preferred_element_type=f32)
+    grad_hid = d_down_in * hidden_part[3]
+    hid_back_one = jnp.sum(grad_hid, axis=-1, keepdims=True) / real
+    hid_back_two = jnp.sum(grad_hid * hidden_hat, axis=-1, keepdims=True) / real
+    d_hidden = (grad_hid - hid_back_one - hidden_hat * hid_back_two) * spread_hid
+    d_gate = (d_hidden * up_pre * sigmoid_gate * (1.0 + gate_pre * (1.0 - sigmoid_gate))).astype(
+        bf16
+    )
+    d_up = (d_hidden * silu_gate).astype(bf16)
+    g_gate_up = jnp.stack(
+        [
+            jnp.einsum("td,tf->df", second_in, d_gate, preferred_element_type=f32).astype(bf16),
+            jnp.einsum("td,tf->df", second_in, d_up, preferred_element_type=f32).astype(bf16),
+        ]
+    )
+    d_second = jnp.einsum("tf,df->td", d_gate, gate_full[0], preferred_element_type=f32)
+    d_second = d_second + jnp.einsum("tf,df->td", d_up, gate_full[1], preferred_element_type=f32)
+    d_resid = cot_rows + norm_back(d_second * norm_scale[1], normed_two, spread_two)
+    d_branch_low = d_resid.astype(bf16)
+    g_out = jnp.einsum("tm,tn->mn", mix_in, d_branch_low, preferred_element_type=f32)
+    d_mix_in = jnp.einsum("tn,mn->tm", d_branch_low, out_full, preferred_element_type=f32)
+    d_mixed = norm_back(d_mix_in * head_part[3], mix_hat, spread_mix).astype(bf16)
+    row_dots = jnp.sum((d_mixed.astype(f32) * mixed).reshape(padded, heads // 2, 2, head_size), axis=-1)
+    row_dots = row_dots.transpose(1, 2, 0)
+    d_query, d_keys, d_values = mix_backward(
+        qkv[0], keys, values, d_mixed, stats, row_dots, key_bias.reshape(-1, 1), head_size
+    )
+
+    def pair_sum(parts):
+        mine = lax.dynamic_slice_in_dim(parts, k * padded, padded, axis=0)
+        yours = lax.dynamic_slice_in_dim(parts, (1 - k) * padded, padded, axis=0)
+        return mine.astype(f32) + lax.ppermute(yours, SHARD, pairs).astype(f32)
+
+    cos, sin = jnp.cos(angles), jnp.sin(angles)
+
+    def turn_back(values):
+        values = values.reshape(padded, heads, head_size)
+        turned = values * cos[:, None] - turn_half(values) * sin[:, None]
+        return turned.reshape(padded, width).astype(bf16)
+
+    d_query_low = turn_back(d_query)
+    d_key_low = turn_back(pair_sum(d_keys))
+    d_value_low = pair_sum(d_values).astype(bf16)
+    g_qkv = jnp.stack(
+        [
+            jnp.einsum("tn,tm->nm", first_in, part, preferred_element_type=f32).astype(bf16)
+            for part in (d_query_low, d_key_low, d_value_low)
+        ]
+    )
+    d_first = jnp.einsum("tm,nm->tn", d_query_low, qkv_full[0], preferred_element_type=f32)
+    d_first = d_first + jnp.einsum("tm,nm->tn", d_key_low, qkv_full[1], preferred_element_type=f32)
+    d_first = d_first + jnp.einsum(
+        "tm,nm->tn", d_value_low, qkv_full[2], preferred_element_type=f32
+    )
+    normed_one, spread_one = standardize(token_rows)
+    d_tokens = d_resid + norm_back(d_first * norm_scale[0], normed_one, spread_one)
+
+    vector_grads = jnp.concatenate(
+        [
+            column_sum(d_query_low),
+            column_sum(d_value_low),
+            column_sum(d_mix_in),
+            column_sum(d_mix_in * mix_hat),
+            column_sum(d_first * normed_one),
+            column_sum(d_second * normed_two),
+            column_sum(d_first),
+            column_sum(d_second),
+            column_sum(d_branch_low),
+            column_sum(cot_block),
+            column_sum(d_gate),
+            column_sum(d_up),
+            column_sum(d_down_in),
+            column_sum(d_down_in * hidden_hat),
+        ]
+    ).reshape(-1, 128)
+    vector_grads = pad_to(vector_grads, 0, round_up(vector_grads.shape[0], 16))
+    grad_jobs = (
+        (0, None, COL, hidden_here // 2), (1, 0, ROW, 64), (1, 1, ROW, 64), (2, None, COL, 256),
+        (3, 0, ROW, 64), (3, 1, ROW, 64), (3, 2, ROW, 64),
+    )
+    down_piece, gate_piece, out_piece, qkv_piece, vector_grads, result, d_tokens = reduce_grads(
+        layers, 1, grad_jobs, (g_down.astype(bf16), g_gate_up, g_out.astype(bf16), g_qkv),
+        vector_grads, (result[:rows], d_tokens[:rows].astype(bf16)),
+    )
+    vector_grads = vector_grads.reshape(-1)
+    head_sums = vector_grads[: 4 * width].reshape(4, heads, head_size)
+    head_sums = lax.dynamic_slice(
+        head_sums, (0, y * heads_here, s * dims_here), (4, heads_here, dims_here)
+    )
+    width_sums = vector_grads[4 * width : 10 * width].reshape(6, width)
+    width_sums = lax.dynamic_slice(width_sums, (0, s * 128), (6, width // shards))
+    hidden_sums = vector_grads[10 * width : 10 * width + 4 * hidden_size]
+    hidden_sums = hidden_sums.reshape(4, hidden_size)
+    hidden_sums = lax.dynamic_slice(hidden_sums, (0, y * hidden_here), (4, hidden_here))
+    hidden_sums = hidden_sums[:, :real_here]
+
+    return (
+        result,
+        d_tokens.astype(f32),
+        qkv_piece,
+        head_sums[:3],
+        head_sums[3],
+        out_piece,
+        width_sums[:2],
+        width_sums[2:],
+        gate_piece[:, :, :real_here],
+        hidden_sums[:3],
+        hidden_sums[3],
+        down_piece[:real_here],
+    )
+
+
 def solution(mesh):
+    small = mesh.shape[CTX] == 2 and mesh.shape[TP] == 2
+    body = functools.partial(image_per_chip, mesh.shape[SHARD] // 2) if small else general_plan
+
     return jax.shard_map(
-        per_device,
+        body,
         mesh=mesh,
         in_specs=(
-            P("shard", "ctx", None),
-            P("shard", "ctx", None),
-            P("shard", None),
-            P(None, "shard", "ctx"),
-            P(None, "shard", "tp"),
-            P(None, "tp", "shard"),
-            P("tp", "shard"),
-            P("tp", "shard"),
-            P(None, "shard"),
-            P(None, "shard"),
-            P(None, "shard", "tp"),
-            P(None, "tp"),
-            P("tp"),
-            P("tp", "shard"),
+            P(SHARD, CTX, None),
+            P(SHARD, CTX, None),
+            P(SHARD, None),
+            P(None, SHARD, CTX),
+            P(None, SHARD, TP),
+            P(None, TP, SHARD),
+            P(TP, SHARD),
+            P(TP, SHARD),
+            P(None, SHARD),
+            P(None, SHARD),
+            P(None, SHARD, TP),
+            P(None, TP),
+            P(TP),
+            P(TP, SHARD),
         ),
         out_specs=(
-            P("shard", "ctx", None),
-            P("shard", "ctx", None),
-            P(None, "shard", "tp"),
-            P(None, "tp", "shard"),
-            P("tp", "shard"),
-            P("tp", "shard"),
-            P(None, "shard"),
-            P(None, "shard"),
-            P(None, "shard", "tp"),
-            P(None, "tp"),
-            P("tp"),
-            P("tp", "shard"),
+            P(SHARD, CTX, None),
+            P(SHARD, CTX, None),
+            P(None, SHARD, TP),
+            P(None, TP, SHARD),
+            P(TP, SHARD),
+            P(TP, SHARD),
+            P(None, SHARD),
+            P(None, SHARD),
+            P(None, SHARD, TP),
+            P(None, TP),
+            P(TP),
+            P(TP, SHARD),
         ),
         check_vma=False,
     )

time: 1660 us -> 616 us (0.37)
  waiting for transfers between devices: 799 us -> 0.01 us
  Pallas kernels: 0 us -> 392 us
  blocking collectives: 219 us -> 0 us
  matrix products: 277 us -> 76.8 us
  local copies, waits for them, and re-layouts: 194 us -> 72.9 us
  other arithmetic: 129 us -> 61.3 us
    pallas_call x0 -> x5, Pallas kernels: none -> 392 us  [the longest x1 185 us: reduce_grads(): pl.pallas_call(functools.partial(reduce_kernel, layers, jobs, len(grads),...]
    psum x7 -> x0, waiting for transfers between devices: 325 us -> none  [the longest x2 122 us: one_batch(): lax.psum(jnp.einsum('htd,hdn->tn', mix_in, out_heads, preferred_element_t...]
    all_gather x12 -> x0, waiting for transfers between devices: 248 us -> none  [the longest x2 117 us: one_batch(): lax.all_gather(gate_up, 'shard', axis=1, tiled=True)]
    dot_general x52 -> x18, matrix products: 256 us -> 76.8 us  [the longest x1 10.9 us: image_per_chip(): jnp.einsum('td,fd->tf', cot_block, down_full, preferred_element_type=f32)]
    while x22 -> x0, waiting for transfers between devices: 107 us -> none
    psum x10 -> x0, blocking collectives: 106 us -> none  [the longest x1 60 us: per_device(): lax.psum((acc_hidden_bias, acc_hidden_scale), ('shard', 'ctx'))]
    all_gather x8 -> x0, blocking collectives: 97.8 us -> none  [the longest x2 30.2 us: one_batch(): lax.all_gather(head_biases, 'shard', axis=2, tiled=True)]
    unnamed x12 -> x0, waiting for transfers between devices: 83.4 us -> none
  transfers between devices with their start and end apart: 27 -> 3, of which waited for: 22 -> 0; matrix products, arithmetic and copies ran while one was open for 17% -> 10% of each run, Pallas kernels for 0% -> 0%
where the time goes in v1:
time: 616 us; the launch traced here: 606 us
  Pallas kernels  392 us (64%)
  matrix products  76.8 us (12%)
  local copies, waits for them, and re-layouts  72.9 us (12%)
  other arithmetic  61.3 us (10%)
    pallas_call x1, Pallas kernels, reduce_grads(): pl.pallas_call(functools.partial(reduce_kernel, layers, jobs, len(grads),...  185 us
    pallas_call x1, Pallas kernels, gather(): pl.pallas_call(functools.partial(gather_kernel, layers, jobs, len(swap_in...  137 us
    pallas_call x1, Pallas kernels, mix_backward(): pl.pallas_call(functools.partial(mix_back_kernel, head_size), grid=(pairs...  34.5 us
    unnamed x119, local copies, waits for them, and re-layouts  23.4 us
    pallas_call x1, Pallas kernels, mix_forward(): pl.pallas_call(functools.partial(mix_kernel, head_size), grid=(pairs,), o...  22.7 us
    reduce_sum x4, other arithmetic, column_sum(): return jnp.sum(values.astype(jnp.float32), axis=0)  16.3 us
    pallas_call x1, Pallas kernels, project(): pl.pallas_call(functools.partial(project_kernel, head_size // 4, tiles),...  13.5 us
  transfers between devices with their start and end apart: 3, of which 0 were waited for; matrix products, arithmetic and copies ran while one was open for 10% of the time, Pallas kernels for 0%

profile of v1, /device:TPU:0, one launch (start us, length us, event | category | flops | bytes accessed | tf_op | source)
XLA Modules:
  0.0 606.3 jit_solution(1727922996627035983)
XLA Ops:
  13.2 136.5 %shard_map.229 = (bf16[3,1024,1024]{2,1,0:T(8,128)(2,1)}, bf16[32,1024]{1,0:T(8,128)(2,1)}, bf16[1024,1024]{1,0:T(8,128)(2,1)}, bf16[2,1024,2816]{2,1,0:T(8,128)...) custom-call(bf16[3,128,512]{2,1,0:T(8,128)(2,1)} %refs_0_.1, ...), custom_call_target="tpu_custom_call" | custom-call | tf_op jit(solution)/shard_map/pallas_call | solution.py:806
  159.5 13.5 %shard_map.230 = (bf16[3,528,1024]{2,1,0:T(8,128)(2,1)}, bf16[528,1024]{1,0:T(8,128)(2,1)}) custom-call(bf16[528,1024]{1,0:T(8,128)(2,1)} %pad.47.x_ref, f32[2,1024]{1,0:T(2,128)} %pad_maximum_fusion.6.norm_ref, bf16[3,1024,1024]{2,1,0:T(8,128)(2,1)} %get-tuple-element.38.w_ref, f32[3,1,1024]{2,1,0:T(1,128)} %broadcast_in_dim.16.bias_ref, ...), custom_call_target="tpu_custom_call" | custom-call | tf_op jit(solution)/shard_map/pallas_call | solution.py:1284
  179.6 3.2 copy.65
  191.9 22.7 %shard_map.231 = (f32[528,1024]{1,0:T(8,128)}, f32[8,2,528]{2,1,0:T(2,128)}) custom-call(bf16[528,1024]{1,0:T(8,128)(2,1)} %slice_bitcast_fusion.q_ref, bf16[1056,1024]{1,0:T(8,128)(2,1)} %bitcast.115, bf16[1056,1024]{1,0:T(8,128)(2,1)} %bitcast.113, f32[1,1056]{1,0:T(1,128)} %reshape.398.bias_ref), custom_call_target="tpu_custom_call" | custom-call | tf_op jit(solution)/shard_map/pallas_call | solution.py:1185
  218.3 3.3 fusion.61
  222.4 3.2 fusion.7
  225.6 6.3 %fusion.56 = (f32[528]{0:T(1024)S(1)}, f32[528,2816]{1,0:T(8,128)S(1)}, f32[528,2816]{1,0:T(8,128)S(1)}) fusion(f32[2816]{0:T(1024)S(1)} %get-tuple-element.114, f32[528,2816]{1,0:T(8,128)S(1)} %fusion.7, f32[2816]{0:T(1024)S(1)} %get-tuple-element.115, bf16[528,1024]{1,0:T(8,128)(2,1)S(1)} %add_convert_fusion.2, bf16[2,1024,2816]{2,1,0:T(8,128)(2,1)} %get-tuple-element.44), kind=kOutput, calls=%fused_computation.186 | convolution fusion | flops 3056958976 | bytes 24715328 | tf_op jit(solution)/shard_map/dot_general | solution.py:1409
  232.7 10.9 %multiply_reduce_fusion = (f32[2816]{0:T(1024)S(1)}, f32[528]{0:T(1024)S(1)}, f32[528]{0:T(1024)S(1)}, f32[2816]{0:T(1024)S(1)}, f32[528,2816]{1,0:T(8,128)}) fusion(f32[528,2816]{1,0:T(8,128)S(1)} %get-tuple-element.130, f32[528]{0:T(1024)S(1)} %add_rsqrt_fusion.1, f32[528]{0:T(1024)S(1)} %broadcast_multiply_fusion.5, f32[2816]{0:T(1024)S(1)} %get-tuple-element.112, ...), kind=kOutput, calls=%fused_computation.2 | convolution fusion | flops 3058439680 | bytes 18760960 | tf_op jit(solution)/shard_map/td,fd->tf/dot_general | solution.py:1424
  243.6 8.6 %convert_reduce_fusion.1 = (f32[2816]{0:T(1024)S(1)}, bf16[528,2816]{1,0:T(8,128)(2,1)}, f32[2816]{0:T(1024)S(1)}, bf16[528,2816]{1,0:T(8,128)(2,1)S(1)}) fusion(f32[528,2816]{1,0:T(8,128)S(1)} %fusion.7, f32[2816]{0:T(1024)S(1)} %get-tuple-element.115, f32[528,2816]{1,0:T(8,128)S(1)} %get-tuple-element.175, f32[2816]{0:T(1024)S(1)} %get-tuple-element.114, ...), kind=kLoop, calls=%fused_computation.4 | loop fusion | flops 38652416 | bytes 29801728 | tf_op jit(solution)/shard_map/reduce_sum | solution.py:60
  252.2 5.4 fusion.1
  257.7 6.8 %multiply_reduce_fusion.5 = (f32[1024]{0:T(1024)}, f32[528]{0:T(1024)S(1)}, f32[528]{0:T(1024)S(1)}, f32[1024]{0:T(1024)S(1)}, f32[528,1024]{1,0:T(8,128)S(1)}) fusion(f32[528,1024]{1,0:T(8,128)S(1)} %get-tuple-element.174, f32[528]{0:T(1024)S(1)} %add_rsqrt_fusion.2, f32[528]{0:T(1024)S(1)} %broadcast_multiply_fusion.13, f32[1024]{0:T(1024)S(1)} %bitcast.131, ...), kind=kOutput, calls=%fused_computation.48 | convolution fusion | flops 3050468352 | bytes 15249664 | tf_op jit(solution)/shard_map/tf,df->td/dot_general | solution.py:1439
  268.5 3.4 convolution_convert_fusion.1.refs_2_
  271.9 6.5 %convert_bitcast_fusion.1 = bf16[1,1024,2816]{2,1,0:T(8,128)(2,1)} fusion(bf16[528,1024]{1,0:T(8,128)(2,1)S(1)} %add_convert_fusion.2, bf16[528,2816]{1,0:T(8,128)(2,1)S(1)} %copy-done.9), kind=kOutput, calls=%fused_computation.22 | convolution fusion | flops 3047948288 | bytes 9822208 | tf_op jit(solution)/shard_map/td,tf->df/dot_general | solution.py:1435
  278.4 6.7 %convert_bitcast_fusion = bf16[1,1024,2816]{2,1,0:T(8,128)(2,1)} fusion(bf16[528,1024]{1,0:T(8,128)(2,1)S(1)} %add_convert_fusion.2, bf16[528,2816]{1,0:T(8,128)(2,1)S(1)} %get-tuple-element.132), kind=kOutput, calls=%fused_computation.21 | convolution fusion | flops 3047948288 | bytes 9822208 | tf_op jit(solution)/shard_map/td,tf->df/dot_general | solution.py:1436
  285.1 4.8 fusion.53
  289.9 2.5 convert_multiply_fusion
  292.4 3.1 copy.63
  295.5 2.6 bitcast_reduce_fusion
  298.1 34.5 %shard_map.232 = (f32[528,1024]{1,0:T(8,128)}, bf16[1056,1024]{1,0:T(8,128)(2,1)}, bf16[1056,1024]{1,0:T(8,128)(2,1)}) custom-call(bf16[528,1024]{1,0:T(8,128)(2,1)} %slice_bitcast_fusion.q_ref, bf16[1056,1024]{1,0:T(8,128)(2,1)} %bitcast.116, bf16[1056,1024]{1,0:T(8,128)(2,1)} %bitcast.114, bf16[528,1024]{1,0:T(8,128)(2,1)} %get-tuple-element.128.do_ref, ...), custom_call_target="tpu_custom_call" | custom-call | tf_op jit(solution)/shard_map/pallas_call | solution.py:1234
  336.7 3.1 copy.66
  339.8 3.2 fusion.20.refs_5_
  343.0 10.2 %pad_maximum_fusion.refs_1_ = bf16[2,1024,2816]{2,1,0:T(8,128)(2,1)} fusion(bf16[1,1024,2816]{2,1,0:T(8,128)(2,1)} %convert_bitcast_fusion, bf16[1,1024,2816]{2,1,0:T(8,128)(2,1)} %convert_bitcast_fusion.1), kind=kLoop, calls=%fused_computation | loop fusion | flops 5767168 | bytes 23068672 | tf_op jit(solution)/shard_map/stack | solution.py:1433
  354.7 6.9 %convolution_convert_fusion.refs_0_ = bf16[2816,1024]{1,0:T(8,128)(2,1)} fusion(bf16[516,1024]{1,0:T(8,128)(2,1)S(1)} %copy-done.21, f32[528,2816]{1,0:T(8,128)S(1)} %bitcast.112, f32[2816]{0:T(1024)S(1)} %copy-done.31, f32[2816]{0:T(1024)S(1)} %get-tuple-element.112, f32[528]{0:T(1024)S(1)} %add_rsqrt_fusion.1, f32[528]{0:T(1024)S(1)} %broadcast_multiply_fusion.5), kind=kOutput, calls=%fused_computation.23 | convolution fusion | flops 3055382528 | bytes 12798080 | tf_op jit(solution)/shard_map/tf,td->fd/dot_general | solution.py:1423
  367.4 2.7 maximum_multiply_fusion
  370.1 3.1 copy.67
  373.2 3.4 copy.70
  376.7 5.0 convert_reduce_fusion.6
  395.0 3.1 pad_maximum_fusion.1.refs_3_
  399.5 184.9 %shard_map.233 = (f32[1408,128]{1,0:T(8,128)}, f32[2,128,1408]{2,1,0:T(8,128)}, f32[512,128]{1,0:T(8,128)}, f32[3,128,512]{2,1,0:T(8,128)}, f32[176,128]{1,0:T(8...) custom-call(bf16[2816,1024]{1,0:T(8,128)(2,1)} %convolution_convert_fusion.refs_0_, ...), custom_call_target="tpu_custom_call" | custom-call | tf_op jit(solution)/shard_map/pallas_call | solution.py:1117
  590.6 5.1 copy.71
  596.6 3.6 copy.73
  600.3 4.2 copy.72
  (232 shorter events, 81.4 us)
Async XLA Ops:
  0.6 8.0 %copy-start.16 = (bf16[2,516,1024]{2,0,1:T(2,128)(2,1)S(1)}, bf16[2,516,1024]{2,0,1:T(2,128)(2,1)}, u32[]{:S(2)}) copy-start(bf16[2,516,1024]{2,0,1:T(2,128)(2,1)} %param.14) | copy-start | bytes 6340612
  158.9 14.1 %copy-start.28 = (f32[1,1024]{1,0:T(1,128)}, f32[1,1024]{1,0:T(1,128)S(1)}, u32[]{:S(2)}) copy-start(f32[1,1024]{1,0:T(1,128)S(1)} %get-tuple-element.179) | copy-start | bytes 12292
  173.0 2.8 copy-start.35
  174.8 12.7 %collective-permute-start = (bf16[2,528,1024]{2,1,0:T(8,128)(2,1)S(1)}, bf16[2,528,1024]{2,1,0:T(8,128)(2,1)}, u32[]{:S(2)}, u32[]{:S(2)}) collective-permute-start(bf16[2,528,1024]{2,1,0:T(8,128)(2,1)S(1)} %slice.191), channel_id=1, source_target_pairs={{0,4},{4,0},{8,12},{12,8},{16,20},{20,16},{24,28},{28,24},{1,5},{5... | collective-permute-start | bytes 6488072 | tf_op jit(solution)/shard_map/ppermute | solution.py:1397
  179.6 3.2 copy-start.3
  182.8 4.7 copy-start.6
  184.1 101.0 %copy-start.30 = (f32[2816]{0:T(1024)}, f32[2816]{0:T(1024)S(1)}, u32[]{:S(2)}) copy-start(f32[2816]{0:T(1024)S(1)} %get-tuple-element.113) | copy-start | bytes 33796
  184.1 5.5 copy-start.26
  214.6 2.3 copy-start.1
  216.9 5.5 slice-start.4
  218.3 4.1 slice-start.5
  218.3 4.1 slice-start.6
  231.9 53.1 %copy-start = (f32[528,2816]{1,0:T(8,128)}, f32[528,2816]{1,0:T(8,128)S(1)}, u32[]{:S(2)}) copy-start(f32[528,2816]{1,0:T(8,128)S(1)} %get-tuple-element.130) | copy-start | bytes 17842180
  252.2 5.5 copy-start.9
  257.7 6.8 %copy-start.20 = (bf16[516,1024]{1,0:T(8,128)(2,1)S(1)}, bf16[516,1024]{1,0:T(8,128)(2,1)}, u32[]{:S(2)}) copy-start(bf16[516,1024]{1,0:T(8,128)(2,1)} %get-tuple-element.46) | copy-start | bytes 3170308
  265.5 3.0 copy-start.7
  271.9 13.2 %slice-start.7 = ((s8[5767168]{0:T(1024)(128)(4,1)}), s8[1572864]{0:T(1024)(128)(4,1)S(1)}, s32[]{:S(2)}) async-start(s8[5767168]{0:T(1024)(128)(4,1)} %bitcast.143), calls=%async_computation.7 | async-start | bytes 3145728
  278.4 6.7 %slice-start.8 = ((s8[5767168]{0:T(1024)(128)(4,1)}), s8[4194304]{0:T(1024)(128)(4,1)S(1)}, s32[]{:S(2)}) async-start(s8[5767168]{0:T(1024)(128)(4,1)} %bitcast.143), calls=%async_computation.8 | async-start | bytes 8388608
  332.6 2.5 copy-start.12
  336.1 52.0 %collective-permute-start.2 = (bf16[528,1024]{1,0:T(8,128)(2,1)}, bf16[528,1024]{1,0:T(8,128)(2,1)}, u32[]{:S(2)}, u32[]{:S(2)}) collective-permute-start(bf16[528,1024]{1,0:T(8,128)(2,1)} %constant_dynamic-slice_fusion.2), channel_id=1, source_target_pairs={{0,4},{4,0},{8,12},{12,8},{16,20},{20,16},{24,28},{28,24},{1,5},{5... | collective-permute-start | bytes 3244040 | tf_op jit(solution)/shard_map/ppermute | solution.py:1455
  336.2 25.4 %collective-permute-start.1 = (bf16[528,1024]{1,0:T(8,128)(2,1)}, bf16[528,1024]{1,0:T(8,128)(2,1)}, u32[]{:S(2)}, u32[]{:S(2)}) collective-permute-start(bf16[528,1024]{1,0:T(8,128)(2,1)} %constant_dynamic-slice_fusion.3), channel_id=1, source_target_pairs={{0,4},{4,0},{8,12},{12,8},{16,20},{20,16},{24,28},{28,24},{1,5},{5... | collective-permute-start | bytes 3244040 | tf_op jit(solution)/shard_map/ppermute | solution.py:1455
  339.8 14.7 %slice-start = ((s8[5947392]{0:T(1024)(128)(4,1)}), s8[4194304]{0:T(1024)(128)(4,1)S(1)}, s32[]{:S(2)}) async-start(s8[5947392]{0:T(1024)(128)(4,1)} %bitcast.111), calls=%async_computation | async-start | bytes 8388608
  343.0 10.2 %copy-start.5 = (f32[528,1024]{0,1:T(8,128)S(1)}, f32[528,1024]{0,1:T(8,128)}, u32[]{:S(2)}) copy-start(f32[528,1024]{0,1:T(8,128)} %copy.66) | copy-start | bytes 6488068
  343.0 11.5 %slice-start.1 = ((s8[5947392]{0:T(1024)(128)(4,1)}), s8[1753088]{0:T(1024)(128)(4,1)S(1)}, s32[]{:S(2)}) async-start(s8[5947392]{0:T(1024)(128)(4,1)} %bitcast.111), calls=%async_computation.1 | async-start | bytes 3506176
  354.7 6.9 %copy-start.14 = (bf16[1056,1024]{1,0:T(8,128)(2,1)S(1)}, bf16[1056,1024]{1,0:T(8,128)(2,1)}, u32[]{:S(2)}) copy-start(bf16[1056,1024]{1,0:T(8,128)(2,1)} %get-tuple-element.51) | copy-start | bytes 6488068
  376.7 5.0 copy-start.39
  381.7 3.7 slice-start.2
  395.0 3.1 copy-start.8
  589.5 6.3 %copy-start.23 = (f32[1408,128]{1,0:T(8,128)S(1)}, f32[1408,128]{1,0:T(8,128)}, u32[]{:S(2)}) copy-start(f32[1408,128]{1,0:T(8,128)} %get-tuple-element.59) | copy-start | bytes 2162692
  595.7 4.5 copy-start.15
  600.3 4.2 copy-start.22
  600.3 5.1 copy-start.24
  (20 other events, 37.2 us)

commit v2 on v1

--- a/solution.py
+++ b/solution.py
@@ -477,6 +477,7 @@
         self.place, self.send_sem, self.recv_sem = place, send_sem, recv_sem
         self.used = 0
         self.sent = []
+        self.noted = None
 
     def take(self, count):
         first = self.used
@@ -493,13 +494,31 @@
             device_id_type=MESH,
         )
 
+    def do(self, condition, action):
+        if self.noted is None:
+            when(condition, action)
+        else:
+            self.noted.append((condition, action))
+
+    def record(self, actions):
+        self.noted = []
+        for action in actions:
+            action()
+        found, self.noted = self.noted, None
+        return found
+
     def send(self, condition, copy):
-        when(condition, copy.start)
+        self.do(condition, copy.start)
         self.sent.append((condition, copy))
 
     def finish(self):
         for condition, copy in self.sent:
             when(condition, copy.wait_send)
+
+
+def run(noted):
+    for condition, action in noted:
+        when(condition, action)
 
 
 def piece_view(kind, rows, cols, ref, y, s, first, size):
@@ -576,14 +595,14 @@
             send(None, self.part_a(CORE, self.core_at(self.core_a, y, z), y, z, True))
         if self.split < self.rows:
             send(None, self.part_b(CORE, self.core_at(self.core_b, y, z), y, z, True))
-        self.local.start()
+        self.links.do(None, self.local.start)
 
     def cross_y(self):
         if self.split == self.rows:
             return
         z, k, x, y = self.links.place
         send = self.links.send
-        self.part_b(BESIDE, self.y_b, 1 - y, z).wait_recv()
+        self.links.do(None, self.part_b(BESIDE, self.y_b, 1 - y, z).wait_recv)
         other = x != y
         low, high = z > 0, z < self.layers - 1
         send(both(other, high), self.part_b(UP, self.z_at(self.z_b, UP, z), 1 - y, z))
@@ -604,13 +623,13 @@
         for way, origin, there, further in self.steps(step):
             if self.split < self.rows:
                 came = self.part_b(way, self.z_at(self.z_b, way, origin), x, origin)
-                when(there, came.wait_recv)
+                self.links.do(there, came.wait_recv)
                 send(both(there, further), came)
                 send(there, self.part_b(ACROSS, self.x_b + origin, x, origin))
                 send(there, self.part_b(CORE, self.core_at(self.core_b, x, origin), x, origin))
             if self.split:
                 came = self.half_a(way, self.z_at(self.z_a, way, origin), y, origin, x)
-                when(there, came.wait_recv)
+                self.links.do(there, came.wait_recv)
                 send(both(there, further), came)
                 send(there, self.half_a(ACROSS, self.x_a + origin, y, origin, x))
 
@@ -619,11 +638,11 @@
         send = self.links.send
         for way, origin, there, further in self.steps(step):
             if self.split:
-                when(there, self.half_a(ACROSS, self.x_a + origin, y, origin, 1 - x).wait_recv)
+                self.links.do(there, self.half_a(ACROSS, self.x_a + origin, y, origin, 1 - x).wait_recv)
                 send(there, self.part_a(BESIDE, self.y_a + origin, y, origin))
                 send(there, self.part_a(CORE, self.core_at(self.core_a, y, origin), y, origin))
             if self.split < self.rows:
-                when(there, self.part_b(ACROSS, self.x_b + origin, 1 - x, origin).wait_recv)
+                self.links.do(there, self.part_b(ACROSS, self.x_b + origin, 1 - x, origin).wait_recv)
                 at = self.core_at(self.core_b, 1 - x, origin)
                 send(there, self.part_b(CORE, at, 1 - x, origin))
 
@@ -634,7 +653,7 @@
         send = self.links.send
         todo = ((None, z, None, None),) if step < 0 else self.steps(step)
         for way, origin, there, further in todo:
-            when(there, self.part_a(BESIDE, self.y_a + origin, 1 - y, origin).wait_recv)
+            self.links.do(there, self.part_a(BESIDE, self.y_a + origin, 1 - y, origin).wait_recv)
             at = self.core_at(self.core_a, 1 - y, origin)
             send(there, self.part_a(CORE, at, 1 - y, origin))
 
@@ -654,25 +673,25 @@
         return found
 
     def arrived(self):
-        self.local.wait()
+        self.links.do(None, self.local.wait)
         for layer in range(self.layers):
             for y in range(2):
                 if self.split:
                     at = self.core_at(self.core_a, y, layer)
-                    self.part_a(CORE, at, y, layer, other_core=True).wait_recv()
+                    self.links.do(None, self.part_a(CORE, at, y, layer, other_core=True).wait_recv)
                 if self.split < self.rows:
                     at = self.core_at(self.core_b, y, layer)
-                    self.part_b(CORE, at, y, layer, other_core=True).wait_recv()
-
-
-def ticks_of(jobs, lead):
+                    self.links.do(None, self.part_b(CORE, at, y, layer, other_core=True).wait_recv)
+
+
+def ticks_of(links, jobs, lead):
     plans = [job.stages() for job in jobs]
     ticks = [[] for _ in range(len(jobs) + max([len(plan) for plan in plans]))]
     for number, plan in enumerate(plans):
         for stage, actions in enumerate(plan):
             at = max(0, number - lead) if stage == 0 else number + stage
             ticks[at] += actions
-    return [tick for tick in ticks if tick]
+    return [links.record(tick) for tick in ticks if tick]
 
 
 class Swap:
@@ -747,74 +766,10 @@
         self.came.wait_recv()
 
 
-def gather_kernel(layers, jobs, swaps, crosses, mats, *refs):
-    own, refs = refs[:mats], refs[mats:]
-    swap_in, refs = refs[:swaps], refs[swaps:]
-    cross_in, refs = refs[:crosses], refs[crosses:]
-    full, refs = refs[:mats], refs[mats:]
-    swap_out, refs = refs[:swaps], refs[swaps:]
-    cross_out, refs = refs[:crosses], refs[crosses:]
-    send_sem, recv_sem, local_sem = refs
-    place = place_of()
-    greet(layers, place, (SWAP,) if swaps else ())
-    links = Links(place, send_sem, recv_sem)
-    y = place[3]
-    extras = []
-    for source, target in zip(swap_in, swap_out):
-        if len(source.shape) > len(target.shape):
-            source = source.at[y]
-        extras.append(Swap(links, source, target, local_sem.at[len(extras)]))
-    for source, target in zip(cross_in, cross_out):
-        extras.append(Cross(links, source, target, local_sem.at[len(extras)]))
-    for extra in extras:
-        extra.begin()
-    todo = []
-    for mat, lead, kind, split in jobs:
-        piece, whole = own[mat], full[mat]
-        if lead is not None:
-            piece, whole = piece.at[lead], whole.at[lead]
-        at = local_sem.at[len(extras) + len(todo)]
-        todo.append(Gather(layers, links, kind, piece, whole, split, at))
-    for tick in ticks_of(todo, 1):
-        for action in tick:
-            action()
-    for job in todo + extras:
-        job.arrived()
-    links.finish()
-
-
 def full_shape(layers, kind, piece):
     if kind == ROW:
         return piece[:-2] + (piece[-2] * layers * 2, piece[-1] * 2)
     return (piece[-2] * 2, piece[-1] * layers * 2)
-
-
-def gather(layers, number, jobs, own, swap_in=(), cross_in=()):
-    kinds = {job[0]: job[2] for job in jobs}
-    shapes = [
-        jax.ShapeDtypeStruct(full_shape(layers, kinds[i], piece.shape), piece.dtype)
-        for i, piece in enumerate(own)
-    ]
-    for item in swap_in:
-        big = item.dtype == jnp.bfloat16
-        shapes.append(jax.ShapeDtypeStruct(item.shape[1:] if big else item.shape, item.dtype))
-    for item in cross_in:
-        shapes.append(jax.ShapeDtypeStruct((2,) + item.shape, item.dtype))
-    extra = len(swap_in) + len(cross_in)
-    sems = len(jobs) * Gather.sem_count(layers) + extra
-    given = list(own) + list(swap_in) + list(cross_in)
-    return pl.pallas_call(
-        functools.partial(gather_kernel, layers, jobs, len(swap_in), len(cross_in), len(own)),
-        out_shape=shapes,
-        in_specs=[ANY] * len(given),
-        out_specs=[ANY] * len(shapes),
-        scratch_shapes=[
-            pltpu.SemaphoreType.DMA((sems,)),
-            pltpu.SemaphoreType.DMA((sems,)),
-            pltpu.SemaphoreType.DMA((len(jobs) + extra,)),
-        ],
-        compiler_params=pltpu.CompilerParams(collective_id=number, has_side_effects=True),
-    )(*given)
 
 
 def by_chunks(shape, body):
@@ -851,7 +806,7 @@
 class Reduce:
     def __init__(self, layers, links, kind, grad, out, split, scratch, local_sem, local_base):
         self.layers, self.links, self.kind, self.grad, self.out = layers, links, kind, grad, out
-        self.mine, self.core_in, self.y_in, self.x_in, self.up_in, self.down_in, self.last = scratch
+        self.mine, self.core_in, self.y_in, self.x_in, self.z_in, self.last = scratch
         self.rows, self.cols = self.mine.shape[-2:]
         self.split = split
         self.local_sem, self.local_base = local_sem, local_base
@@ -878,6 +833,9 @@
     def part_b(self, ref):
         return cut_rows(ref, self.split, self.rows - self.split)
 
+    def add(self, condition, target, term):
+        self.links.do(condition, functools.partial(add_into, target, term))
+
     def grad_piece(self, y, s):
         return piece_view(self.kind, self.rows, self.cols, self.grad, y, s, 0, self.rows)
 
@@ -902,7 +860,7 @@
         for layer in self.order:
             for y in range(2):
                 self.links.send(None, self.to_core(y, layer))
-                self.local(y, layer).start()
+                self.links.do(None, self.local(y, layer).start)
 
     def to_y(self, layer):
         y = self.links.place[3]
@@ -917,34 +875,34 @@
     def chip_sum(self):
         for layer in self.order:
             for side in range(2):
-                self.local(side, layer).wait()
-                self.to_core(side, layer).wait_recv()
-                add_into(self.mine.at[side, layer], self.core_in.at[side, layer])
+                self.links.do(None, self.local(side, layer).wait)
+                self.links.do(None, self.to_core(side, layer).wait_recv)
+                self.add(None, self.mine.at[side, layer], self.core_in.at[side, layer])
             self.links.send(None, self.to_y(layer))
             self.links.send(None, self.to_x(layer))
 
     def plane_sum(self):
         z, k, x, y = self.links.place
         for layer in self.order:
-            self.to_y(layer).wait_recv()
-            add_into(self.part_a(self.mine.at[y, layer]), self.y_in.at[layer])
-            self.to_x(layer).wait_recv()
-            add_into(self.part_b(self.mine.at[x, layer]), self.x_in.at[layer])
-
-    def chain(self, way, layer):
+            self.links.do(None, self.to_y(layer).wait_recv)
+            self.add(None, self.part_a(self.mine.at[y, layer]), self.y_in.at[layer])
+            self.links.do(None, self.to_x(layer).wait_recv)
+            self.add(None, self.part_b(self.mine.at[x, layer]), self.x_in.at[layer])
+
+    def chain(self, way, layer, receiver):
         z, k, x, y = self.links.place
-        inbox = self.up_in if way == UP else self.down_in
+        slot = layer if way == UP else jnp.where(receiver == layer, self.layers, layer)
         add = 0 if way == UP else self.layers
         found = []
         for base, part, side in ((self.z_a, self.part_a, y), (self.z_b, self.part_b, x)):
-            total, box = part(self.mine.at[side, layer]), part(inbox.at[layer])
+            total, box = part(self.mine.at[side, layer]), part(self.z_in.at[slot])
             found.append((total, box, self.links.copy(way, base + add + layer, total, box)))
         return found
 
-    def take(self, way, layer):
-        for total, box, copy in self.chain(way, layer):
-            copy.wait_recv()
-            add_into(total, box)
+    def take(self, condition, way, layer):
+        for total, box, copy in self.chain(way, layer, self.links.place[0]):
+            self.links.do(condition, copy.wait_recv)
+            self.add(condition, total, box)
 
     def along_z(self, depth):
         z = self.links.place[0]
@@ -955,14 +913,14 @@
         ):
             for layer in goals:
                 if depth:
-                    pl.when(here)(functools.partial(self.take, way, layer))
-                for total, box, copy in self.chain(way, layer):
+                    self.take(here, way, layer)
+                for total, box, copy in self.chain(way, layer, z + 1 if way == UP else z - 1):
                     self.links.send(here, copy)
 
     def ending(self):
         z, k, x, y = self.links.place
-        pl.when(z > 0)(functools.partial(self.take, UP, z))
-        pl.when(z < self.layers - 1)(functools.partial(self.take, DOWN, z))
+        self.take(z > 0, UP, z)
+        self.take(z < self.layers - 1, DOWN, z)
         self.sum_a, self.sum_b = self.part_a(self.mine.at[y, z]), self.part_b(self.mine.at[x, z])
         self.got_a, self.got_b = self.part_a(self.last.at[0]), self.part_b(self.last.at[0])
         self.got_y = self.part_b(self.last.at[1])
@@ -975,25 +933,20 @@
     def owner(self):
         z, k, x, y = self.links.place
 
-        def own():
-            self.y_end.wait_recv()
-            add_into(self.sum_b, self.got_y)
-
-        pl.when(y == x)(own)
+        self.links.do(y == x, self.y_end.wait_recv)
+        self.add(y == x, self.sum_b, self.got_y)
         self.links.send(y == x, self.x_last)
-        self.x_end.wait_recv()
-        store_sum(self.part_a(self.out), self.sum_a, self.got_a)
+        self.links.do(None, self.x_end.wait_recv)
+        out_a = self.part_a(self.out)
+        self.links.do(None, functools.partial(store_sum, out_a, self.sum_a, self.got_a))
 
     def write(self):
         z, k, x, y = self.links.place
         out_b = self.part_b(self.out)
 
-        def received():
-            self.x_last.wait_recv()
-            store_sum(out_b, self.got_b)
-
-        pl.when(y != x)(received)
-        pl.when(y == x)(lambda: store_sum(out_b, self.sum_b))
+        self.links.do(y != x, self.x_last.wait_recv)
+        self.links.do(y != x, functools.partial(store_sum, out_b, self.got_b))
+        self.links.do(y == x, functools.partial(store_sum, out_b, self.sum_b))
 
     def stages(self):
         chains = [[functools.partial(self.along_z, depth)] for depth in range(self.layers - 1)]
@@ -1024,10 +977,10 @@
 
     def join(self, number):
         z = self.links.place[0]
-        self.exchange(number).wait_recv()
+        self.links.do(None, self.exchange(number).wait_recv)
         mine = self.given if number == 0 else self.boxes.at[2 + number]
         result = self.layer_boxes.at[z] if number == 2 else self.boxes.at[3 + number]
-        store_sum(result, mine, self.boxes.at[number])
+        self.links.do(None, functools.partial(store_sum, result, mine, self.boxes.at[number]))
         if number < 2:
             self.links.send(None, self.exchange(number + 1))
         else:
@@ -1047,16 +1000,41 @@
             (DOWN, above, above <= top, z > 0),
         ):
             copy = self.pass_on(way, origin)
-            when(there, copy.wait_recv)
+            self.links.do(there, copy.wait_recv)
             self.links.send(both(there, further), copy)
 
     def write(self):
-        store_sum(self.out, *[self.layer_boxes.at[layer] for layer in range(self.layers)])
+        layers = [self.layer_boxes.at[layer] for layer in range(self.layers)]
+        self.links.do(None, functools.partial(store_sum, self.out, *layers))
 
     def stages(self):
         joins = [[functools.partial(self.join, number)] for number in range(3)]
         moves = [[functools.partial(self.along_z, step)] for step in range(self.layers - 1)]
         return [[self.begin], *joins, *moves, [self.write]]
+
+
+def reduce_jobs(layers, links, jobs, grads, outs, scratch, local_sem):
+    todo = []
+    for number, (mat, lead, kind, split) in enumerate(jobs):
+        grad, out = grads[mat], outs[mat]
+        if lead is not None:
+            grad, out = grad.at[lead], out.at[lead]
+        own = scratch[6 * number : 6 * number + 6]
+        at = number * 2 * layers
+        todo.append(Reduce(layers, links, kind, grad, out, split, own, local_sem, at))
+    return todo
+
+
+def reduce_scratch(layers, jobs, pieces):
+    scratch = []
+    for mat, lead, kind, split in jobs:
+        rows, cols = pieces[mat][-2:]
+        for lead_shape, here in (
+            ((2, layers), rows), ((2, layers), rows), ((layers,), split), ((layers,), rows - split),
+            ((layers + 1,), rows), ((2,), rows),
+        ):
+            scratch.append(pltpu.VMEM(lead_shape + (here, cols), jnp.bfloat16))
+    return scratch
 
 
 def reduce_kernel(layers, jobs, mats, blocks, *refs):
@@ -1066,28 +1044,20 @@
     outs, refs = refs[:mats], refs[mats:]
     total_out, refs = refs[0], refs[1:]
     block_out, refs = refs[:blocks], refs[blocks:]
-    scratch = refs[: 7 * len(jobs)]
-    boxes, layer_boxes, send_sem, recv_sem, local_sem = refs[7 * len(jobs) :]
+    scratch = refs[: 6 * len(jobs)]
+    boxes, layer_boxes, send_sem, recv_sem, local_sem = refs[6 * len(jobs) :]
     place = place_of()
     greet(layers, place, (SWAP, FAR))
     links = Links(place, send_sem, recv_sem)
-    todo = []
-    for number, (mat, lead, kind, split) in enumerate(jobs):
-        grad, out = grads[mat], outs[mat]
-        if lead is not None:
-            grad, out = grad.at[lead], out.at[lead]
-        own = scratch[7 * number : 7 * number + 7]
-        at = number * 2 * layers
-        todo.append(Reduce(layers, links, kind, grad, out, split, own, local_sem, at))
+    todo = reduce_jobs(layers, links, jobs, grads, outs, scratch, local_sem)
     todo.insert(1, Total(layers, links, total_in, total_out, boxes, layer_boxes))
     extras = [
         Spread(links, source, target, local_sem.at[len(jobs) * 2 * layers + i])
         for i, (source, target) in enumerate(zip(block_in, block_out))
     ]
-    for number, tick in enumerate(ticks_of(todo, 1)):
-        for action in tick:
-            action()
-        if number == 2:
+    for number, tick in enumerate(ticks_of(links, todo, 1)):
+        run(tick)
+        if number == 0:
             for extra in extras:
                 extra.begin()
     for extra in extras:
@@ -1104,14 +1074,7 @@
 def reduce_grads(layers, number, jobs, grads, total, blocks):
     kinds = {job[0]: job[2] for job in jobs}
     pieces = [piece_shape(layers, kinds[i], g.shape) for i, g in enumerate(grads)]
-    scratch = []
-    for mat, lead, kind, split in jobs:
-        rows, cols = pieces[mat][-2:]
-        for lead_shape, here in (
-            ((2, layers), rows), ((2, layers), rows), ((layers,), split), ((layers,), rows - split),
-            ((layers,), rows), ((layers,), rows), ((2,), rows),
-        ):
-            scratch.append(pltpu.VMEM(lead_shape + (here, cols), jnp.bfloat16))
+    scratch = reduce_scratch(layers, jobs, pieces)
     sems = len(jobs) * Reduce.sem_count(layers) + Total.sem_count(layers) + 2 * len(blocks)
     images = [jax.ShapeDtypeStruct((2,) + block.shape, block.dtype) for block in blocks]
     return pl.pallas_call(
@@ -1161,93 +1124,6 @@
 LOG2_E = 1.4426950408889634
 
 
-def mix_kernel(head_size, q_ref, k_ref, v_ref, bias_ref, o_ref, stat_ref):
-    scale = LOG2_E / math.sqrt(head_size)
-    q, k, v = q_ref[...], k_ref[...], v_ref[...]
-    bias = bias_ref[...]
-    parts = []
-    for head in range(2):
-        s = dot_last(only_head(q, head, head_size), k) * scale + bias
-        top = jnp.max(s, axis=1, keepdims=True)
-        e = jnp.exp2(s - top)
-        total = jnp.sum(e, axis=1, keepdims=True)
-        parts.append(dot(e.astype(jnp.bfloat16), v) * (1.0 / total))
-        level = jnp.broadcast_to(top + jnp.log2(total), (q.shape[0], 128))
-        stat_ref[0, head : head + 1, :] = jnp.transpose(level)[0:1, :]
-    o_ref[...] = jnp.where(pair_lanes(o_ref.shape, head_size), parts[0], parts[1])
-
-
-def mix_forward(q, k, v, bias, head_size):
-    rows, width = q.shape
-    keys = k.shape[0]
-    pairs = width // (2 * head_size)
-    lanes = 2 * head_size
-    return pl.pallas_call(
-        functools.partial(mix_kernel, head_size),
-        grid=(pairs,),
-        out_shape=[
-            jax.ShapeDtypeStruct((rows, width), jnp.float32),
-            jax.ShapeDtypeStruct((pairs, 2, rows), jnp.float32),
-        ],
-        in_specs=[
-            pl.BlockSpec((rows, lanes), lambda i: (0, i)),
-            pl.BlockSpec((keys, lanes), lambda i: (0, i)),
-            pl.BlockSpec((keys, lanes), lambda i: (0, i)),
-            pl.BlockSpec((1, keys), lambda i: (0, 0)),
-        ],
-        out_specs=[
-            pl.BlockSpec((rows, lanes), lambda i: (0, i)),
-            pl.BlockSpec((1, 2, rows), lambda i: (i, 0, 0)),
-        ],
-        compiler_params=pltpu.CompilerParams(vmem_limit_bytes=LIMIT),
-    )(q, k, v, bias)
-
-
-def mix_back_kernel(
-    head_size, q_ref, k_ref, v_ref, do_ref, stat_ref, dot_ref, bias_ref, dq_ref, dk_ref, dv_ref
-):
-    scale = 1.0 / math.sqrt(head_size)
-    q, k, v, do = q_ref[...], k_ref[...], v_ref[...], do_ref[...]
-    bias = bias_ref[...]
-    found = []
-    for head in range(2):
-        s = dot_last(k, only_head(q, head, head_size)) * (scale * LOG2_E) + bias
-        p = jnp.exp2(s - stat_ref[0, head : head + 1, :])
-        dp = dot_last(v, only_head(do, head, head_size))
-        ds = (p * (dp - dot_ref[0, head : head + 1, :])).astype(jnp.bfloat16)
-        dv = dot(p.astype(jnp.bfloat16), do)
-        dk = dot(ds, q) * scale
-        dq = dot_first(ds, k) * scale
-        found.append((dq, dk, dv))
-    for ref, first, second in zip((dq_ref, dk_ref, dv_ref), *found):
-        ref[...] = jnp.where(pair_lanes(ref.shape, head_size), first, second).astype(ref.dtype)
-
-
-def mix_backward(q, k, v, do, stats, row_dots, bias, head_size):
-    rows, width = q.shape
-    keys = k.shape[0]
-    pairs = width // (2 * head_size)
-    lanes = 2 * head_size
-    of_rows = pl.BlockSpec((rows, lanes), lambda i: (0, i))
-    of_keys = pl.BlockSpec((keys, lanes), lambda i: (0, i))
-    of_stats = pl.BlockSpec((1, 2, rows), lambda i: (i, 0, 0))
-    return pl.pallas_call(
-        functools.partial(mix_back_kernel, head_size),
-        grid=(pairs,),
-        out_shape=[
-            jax.ShapeDtypeStruct((rows, width), jnp.float32),
-            jax.ShapeDtypeStruct((keys, width), jnp.bfloat16),
-            jax.ShapeDtypeStruct((keys, width), jnp.bfloat16),
-        ],
-        in_specs=[
-            of_rows, of_keys, of_keys, of_rows, of_stats, of_stats,
-            pl.BlockSpec((keys, 1), lambda i: (0, 0)),
-        ],
-        out_specs=[of_rows, of_keys, of_keys],
-        compiler_params=pltpu.CompilerParams(vmem_limit_bytes=LIMIT),
-    )(q, k, v, do, stats, row_dots, bias)
-
-
 def turn_lanes(values, quarter):
     width = values.shape[-1]
     lane = lax.broadcasted_iota(jnp.int32, (1, width), 1)
@@ -1257,51 +1133,353 @@
     return jnp.where(even, -after, before)
 
 
-def project_kernel(quarter, tiles, x_ref, norm_ref, w_ref, bias_ref, cos_ref, sin_ref, out_ref, n_ref):
-    step = pl.program_id(0)
-
-    @pl.when(step == 0)
-    def _():
-        hat, spread = standardize(x_ref[...].astype(jnp.float32))
-        n_ref[...] = (hat * norm_ref[0:1, :] + norm_ref[1:2, :]).astype(jnp.bfloat16)
-
-    raw = dot(n_ref[...], w_ref[0]) + bias_ref[0]
-
-    @pl.when(step < 2 * tiles)
-    def _():
-        turned = turn_lanes(raw, quarter)
-        out_ref[0] = (raw * cos_ref[...] + turned * sin_ref[...]).astype(jnp.bfloat16)
-
-    @pl.when(step >= 2 * tiles)
-    def _():
-        out_ref[0] = raw.astype(jnp.bfloat16)
-
-
-def project(x, norm, weights, bias, cos, sin, head_size, tile=256):
+def front_kernel(layers, head_size, grid_side, *refs):
+    (
+        vec_own, qkv_own, out_own, gate_own, down_own, tokens, valid, hidden_own,
+        vec_full, qkv_full, out_full, gate_full, down_full, hidden_full,
+        x_out, n_out, q_out, k_out, v_out, o_out, stat_out, vec_out, count_out,
+        x, valid_both, vec, weight, hat, normed, q, keys, values, cos, sin, bias,
+        send_sem, recv_sem, local_sem,
+    ) = refs
+    f32, bf16 = jnp.float32, jnp.bfloat16
+    place = place_of()
+    z, k, me_x, y = place
+    greet(layers, place, (SWAP,))
+    links = Links(place, send_sem, recv_sem)
     rows, width = x.shape
-    tiles = width // tile
-    fixed = lambda i: (0, 0)
+    tokens_here = valid.shape[1] // 2
+    tile = weight.shape[2]
+    quarter = head_size // 4
+    lanes = 2 * head_size
+    locals_used = [0]
+
+    def local_at():
+        locals_used[0] += 1
+        return local_sem.at[locals_used[0] - 1]
+
+    block = Swap(links, tokens.at[y], x, local_at())
+    valid_swap = Swap(links, valid, valid_both, local_at())
+    cross = Cross(links, hidden_own, hidden_full, local_at())
+    half = out_own.shape[0] // 2
+    down_half = down_own.shape[0] // 2
+    todo = [
+        (ROW, vec_own, vec_full, 0),
+        (ROW, qkv_own.at[0], qkv_full.at[0], 64),
+        (ROW, qkv_own.at[1], qkv_full.at[1], 64),
+        (ROW, qkv_own.at[2], qkv_full.at[2], 64),
+        (COL, out_own, out_full, half),
+        (ROW, gate_own.at[0], gate_full.at[0], 64),
+        (ROW, gate_own.at[1], gate_full.at[1], 64),
+        (COL, down_own, down_full, down_half),
+    ]
+    jobs = [
+        Gather(layers, links, kind, own, full, split, local_at())
+        for kind, own, full, split in todo
+    ]
+    ticks = ticks_of(links, jobs, 1)
+    weight_loads = []
+    for mat in range(3):
+        for part in range(width // tile):
+            slot = len(weight_loads) % 2
+            weight_loads.append(
+                pltpu.make_async_copy(
+                    qkv_full.at[mat, :, pl.ds(part * tile, tile)], weight.at[slot], local_at()
+                )
+            )
+    vec_load = pltpu.make_async_copy(vec_full, vec, local_at())
+    keeps = [
+        pltpu.make_async_copy(source, target, local_at())
+        for source, target in ((x, x_out), (normed, n_out), (q, q_out), (keys, k_out), (values, v_out))
+    ]
+    shares = []
+    my_rows = pl.ds(pl.multiple_of(k * rows, 16), rows)
+    other_rows = pl.ds(pl.multiple_of((1 - k) * rows, 16), rows)
+    for store in (keys, values):
+        for part in range(width // tile):
+            at = links.take(1)
+            cols = pl.ds(part * tile, tile)
+            out_going = links.copy(CORE, at, store.at[my_rows, cols], store.at[my_rows, cols])
+            coming = links.copy(CORE, at, store.at[other_rows, cols], store.at[other_rows, cols])
+            shares.append((out_going, coming))
+
+    block.begin()
+    valid_swap.begin()
+    run(ticks[0])
+    cross.begin()
+    run(ticks[1])
+
+    block.arrived()
+    valid_swap.arrived()
+    keeps[0].start()
+    chunk = rows // 3
+
+    def normalise(i, nothing):
+        at = pl.ds(pl.multiple_of(i * chunk, 16), chunk)
+        value, spread = standardize(x[at, :].astype(f32))
+        hat[at, :] = value
+        return nothing
+
+    lax.fori_loop(0, 3, normalise, 0)
+    flags = jnp.where(y == 0, valid_both[0:1, :], valid_both[1:2, :]).astype(f32)
+    count = jnp.sum(flags, axis=1, keepdims=True)
+    count_out[...] = jnp.broadcast_to(count, count_out.shape)
+    columns = (count - 1.0) * (1.0 / grid_side)
+    token = lax.broadcasted_iota(jnp.int32, (rows, lanes), 0).astype(f32)
+    token = token + (k * tokens_here).astype(f32)
+    lane = lax.broadcasted_iota(jnp.int32, (rows, lanes), 1)
+    live = jnp.logical_and(token >= 1.0, token < count)
+    row_id = jnp.floor((token - 0.5) / columns)
+    col_id = token - 1.0 - row_id * columns
+    where_at = jnp.where(lax.rem(lane, head_size) < 2 * quarter, row_id, col_id)
+    where_at = jnp.where(live, where_at, 0.0)
+    power = lax.rem(lane, quarter).astype(f32) * (-math.log(10000.0) / quarter)
+    angle = where_at * jnp.exp(power)
+    cos[...] = jnp.cos(angle)
+    sin[...] = jnp.sin(angle)
+    key = lax.broadcasted_iota(jnp.int32, bias.shape, 1)
+    second = key >= rows
+    within = jnp.where(second, key - rows, key)
+    key_token = jnp.where(second, within + tokens_here, within).astype(f32)
+    seen = jnp.logical_and(within < tokens_here, key_token < count)
+    bias[...] = jnp.where(seen, 0.0, -1e30)
+
+    for tick in ticks[2:8]:
+        run(tick)
+    jobs[0].arrived()
+    vec_load.start()
+    vec_load.wait()
+    piece_rows = vec_own.shape[0]
+    summed = vec[0:piece_rows, :].astype(f32)
+    for s in range(1, 2 * layers):
+        summed = summed + vec[s * piece_rows : (s + 1) * piece_rows, :].astype(f32)
+    vec_out[...] = summed
+
+    def scale(i, nothing):
+        at = pl.ds(pl.multiple_of(i * chunk, 16), chunk)
+        normed[at, :] = (hat[at, :] * vec_out[4:5, :] + vec_out[6:7, :]).astype(bf16)
+        return nothing
+
+    lax.fori_loop(0, 3, scale, 0)
+    keeps[1].start()
+    run(ticks[8])
+    repeat = tile // lanes
+    per = width // tile
+    for mat in range(3):
+        jobs[1 + mat].arrived()
+        for part in range(per):
+            weight_loads[mat * per + part].start()
+        for part in range(per):
+            load = weight_loads[mat * per + part]
+            load.wait()
+            cols = pl.ds(part * tile, tile)
+            raw = dot(normed[...], weight[(mat * per + part) % 2])
+            if mat != 1:
+                raw = raw + vec_out[0 if mat == 0 else 1 : 1 if mat == 0 else 2, cols]
+            if mat < 2:
+                turned = turn_lanes(raw, quarter)
+                wide_cos = jnp.concatenate([cos[...]] * repeat, axis=1)
+                wide_sin = jnp.concatenate([sin[...]] * repeat, axis=1)
+                raw = raw * wide_cos + turned * wide_sin
+            if mat == 0:
+                q[:, cols] = raw.astype(bf16)
+            else:
+                (keys if mat == 1 else values)[my_rows, cols] = raw.astype(bf16)
+                shares[(mat - 1) * per + part][0].start()
+        run(ticks[9 + mat])
+    keeps[2].start()
+    for out_going, coming in shares:
+        out_going.wait_send()
+        coming.wait_recv()
+    keeps[3].start()
+    keeps[4].start()
+
+    late = ticks[12:]
+    score_scale = LOG2_E / math.sqrt(head_size)
+    pairs = width // lanes
+
+    def mix(i, nothing):
+        for number, tick in enumerate(late):
+            pl.when(i == number)(functools.partial(run, tick))
+        cols = pl.ds(pl.multiple_of(i * lanes, lanes), lanes)
+        queries, near_keys, near_values = q[:, cols], keys[:, cols], values[:, cols]
+        parts = []
+        for head in range(2):
+            s = dot_last(only_head(queries, head, head_size), near_keys) * score_scale + bias[...]
+            top = jnp.max(s, axis=1, keepdims=True)
+            e = jnp.exp2(s - top)
+            total = jnp.sum(e, axis=1, keepdims=True)
+            parts.append(dot(e.astype(bf16), near_values) * (1.0 / total))
+            level = jnp.broadcast_to(top + jnp.log2(total), (rows, 128))
+            stat_out[i, head : head + 1, :] = jnp.transpose(level)[0:1, :]
+        o_out[:, cols] = jnp.where(pair_lanes((rows, lanes), head_size), parts[0], parts[1])
+        return nothing
+
+    lax.fori_loop(0, pairs, mix, 0)
+    for tick in late[8:]:
+        run(tick)
+    for job in jobs[4:]:
+        job.arrived()
+    cross.arrived()
+    for keep in keeps:
+        keep.wait()
+    links.finish()
+
+
+def front(layers, number, head_size, grid_side, vec, qkv, out, gate, down, tokens, valid, hidden):
+    bf16, f32 = jnp.bfloat16, jnp.float32
+    rows, width = tokens.shape[1:]
+    pairs = width // (2 * head_size)
+    tile = 512
+    fulls = [
+        full_shape(layers, kind, piece.shape)
+        for kind, piece in ((ROW, vec), (ROW, qkv), (COL, out), (ROW, gate), (COL, down))
+    ]
+    shapes = [jax.ShapeDtypeStruct(shape, bf16) for shape in fulls]
+    shapes += [jax.ShapeDtypeStruct((2,) + hidden.shape, bf16)]
+    shapes += [jax.ShapeDtypeStruct((n * rows, width), bf16) for n in (1, 1, 1, 2, 2)]
+    shapes += [
+        jax.ShapeDtypeStruct((rows, width), f32),
+        jax.ShapeDtypeStruct((pairs, 2, rows), f32),
+        jax.ShapeDtypeStruct((vec.shape[0], width), f32),
+        jax.ShapeDtypeStruct((8, 128), f32),
+    ]
+    sems = 8 * Gather.sem_count(layers) + 7
     return pl.pallas_call(
-        functools.partial(project_kernel, head_size // 4, tiles),
-        grid=(3 * tiles,),
-        out_shape=[
-            jax.ShapeDtypeStruct((3, rows, width), jnp.bfloat16),
-            jax.ShapeDtypeStruct((rows, width), jnp.bfloat16),
+        functools.partial(front_kernel, layers, head_size, grid_side),
+        out_shape=shapes,
+        in_specs=[ANY] * 8,
+        out_specs=[ANY] * 11 + [IN_VMEM] * 4,
+        scratch_shapes=[
+            pltpu.VMEM((rows, width), bf16),
+            pltpu.VMEM(valid.shape, valid.dtype),
+            pltpu.VMEM(fulls[0], bf16),
+            pltpu.VMEM((2, width, tile), bf16),
+            pltpu.VMEM((rows, width), f32),
+            pltpu.VMEM((rows, width), bf16),
+            pltpu.VMEM((rows, width), bf16),
+            pltpu.VMEM((2 * rows, width), bf16),
+            pltpu.VMEM((2 * rows, width), bf16),
+            pltpu.VMEM((rows, 2 * head_size), f32),
+            pltpu.VMEM((rows, 2 * head_size), f32),
+            pltpu.VMEM((1, 2 * rows), f32),
+            pltpu.SemaphoreType.DMA((sems,)),
+            pltpu.SemaphoreType.DMA((sems,)),
+            pltpu.SemaphoreType.DMA((32,)),
         ],
-        in_specs=[
-            pl.BlockSpec((rows, width), fixed),
-            pl.BlockSpec((2, width), fixed),
-            pl.BlockSpec((1, width, tile), lambda i: (i // tiles, 0, i % tiles)),
-            pl.BlockSpec((1, 1, tile), lambda i: (i // tiles, 0, i % tiles)),
-            pl.BlockSpec((rows, tile), fixed),
-            pl.BlockSpec((rows, tile), fixed),
+        compiler_params=pltpu.CompilerParams(
+            collective_id=number, has_side_effects=True, vmem_limit_bytes=LIMIT
+        ),
+    )(vec, qkv, out, gate, down, tokens, valid, hidden)
+
+
+def back_kernel(layers, head_size, jobs, mats, *refs):
+    grads, refs = refs[:mats], refs[mats:]
+    q, keys, values, do, stats, row_dots, bias, cos, sin = refs[:9]
+    outs, refs = refs[9 : 9 + mats], refs[9 + mats :]
+    dq_out, dk_out, dv_out = refs[:3]
+    scratch, refs = refs[3 : 3 + 6 * len(jobs)], refs[3 + 6 * len(jobs) :]
+    k_box, v_box, k_sum, v_sum, send_sem, recv_sem, local_sem = refs
+    f32, bf16 = jnp.float32, jnp.bfloat16
+    place = place_of()
+    z, k, x, y = place
+    greet(layers, place, ())
+    links = Links(place, send_sem, recv_sem)
+    todo = reduce_jobs(layers, links, jobs, grads, outs, scratch, local_sem)
+    ticks = ticks_of(links, todo, 1)
+    rows, width = q.shape
+    lanes = 2 * head_size
+    pairs = width // lanes
+    scale = 1.0 / math.sqrt(head_size)
+    quarter = head_size // 4
+    my_rows = pl.ds(pl.multiple_of(k * rows, 16), rows)
+    other_rows = pl.ds(pl.multiple_of((1 - k) * rows, 16), rows)
+    first = links.take(2 * pairs)
+
+    def share(i):
+        cols = pl.ds(pl.multiple_of(i * lanes, lanes), lanes)
+        return (
+            links.copy(CORE, first + 2 * i, k_sum.at[other_rows, cols], k_box.at[:, cols]),
+            links.copy(CORE, first + 2 * i + 1, v_sum.at[other_rows, cols], v_box.at[:, cols]),
+        )
+
+    def turn_back(grad):
+        return grad * cos[...] - turn_lanes(grad, quarter) * sin[...]
+
+    lead = 2
+    for tick in ticks[:lead]:
+        run(tick)
+    late = ticks[lead:]
+
+    def step(i, nothing):
+        for number, tick in enumerate(late[:pairs]):
+            pl.when(i == number)(functools.partial(run, tick))
+        cols = pl.ds(pl.multiple_of(i * lanes, lanes), lanes)
+        queries, near_keys, near_values, grad = q[:, cols], keys[:, cols], values[:, cols], do[:, cols]
+        found = []
+        for head in range(2):
+            s = dot_last(near_keys, only_head(queries, head, head_size)) * (scale * LOG2_E)
+            p = jnp.exp2(s + bias[...] - stats[i, head : head + 1, :])
+            dp = dot_last(near_values, only_head(grad, head, head_size))
+            ds = (p * (dp - row_dots[i, head : head + 1, :])).astype(bf16)
+            found.append(
+                (dot_first(near_keys, ds) * scale, dot(ds, queries) * scale, dot(p.astype(bf16), grad))
+            )
+        dq = jnp.concatenate([found[0][0][:head_size], found[1][0][head_size:]], axis=0)
+        dq_out[:, cols] = turn_back(jnp.transpose(dq)).astype(bf16)
+        in_first = pair_lanes((2 * rows, lanes), head_size)
+        k_sum[:, cols] = jnp.where(in_first, found[0][1], found[1][1]).astype(bf16)
+        v_sum[:, cols] = jnp.where(in_first, found[0][2], found[1][2]).astype(bf16)
+        for copy in share(i):
+            copy.start()
+        return nothing
+
+    lax.fori_loop(0, pairs, step, 0)
+
+    def join(i, nothing):
+        cols = pl.ds(pl.multiple_of(i * lanes, lanes), lanes)
+        for copy in share(i):
+            copy.wait()
+        dk = k_sum[my_rows, cols].astype(f32) + k_box[:, cols].astype(f32)
+        dk_out[:, cols] = turn_back(dk).astype(bf16)
+        dv = v_sum[my_rows, cols].astype(f32) + v_box[:, cols].astype(f32)
+        dv_out[:, cols] = dv.astype(bf16)
+        return nothing
+
+    for tick in late[pairs : pairs + 1]:
+        run(tick)
+    lax.fori_loop(0, pairs, join, 0)
+    for tick in late[pairs + 1 :]:
+        run(tick)
+    links.finish()
+
+
+def back(layers, number, head_size, jobs, grads, q, keys, values, do, stats, row_dots, bias, cos, sin):
+    bf16, f32 = jnp.bfloat16, jnp.float32
+    kinds = {job[0]: job[2] for job in jobs}
+    pieces = [piece_shape(layers, kinds[i], g.shape) for i, g in enumerate(grads)]
+    rows, width = q.shape
+    pairs = width // (2 * head_size)
+    sems = len(jobs) * Reduce.sem_count(layers) + 2 * pairs
+    return pl.pallas_call(
+        functools.partial(back_kernel, layers, head_size, jobs, len(grads)),
+        out_shape=[jax.ShapeDtypeStruct(piece, f32) for piece in pieces]
+        + [jax.ShapeDtypeStruct((rows, width), bf16) for _ in range(3)],
+        in_specs=[ANY] * len(grads) + [IN_VMEM] * 9,
+        out_specs=[IN_VMEM] * (len(pieces) + 3),
+        scratch_shapes=reduce_scratch(layers, jobs, pieces)
+        + [
+            pltpu.VMEM((rows, width), bf16),
+            pltpu.VMEM((rows, width), bf16),
+            pltpu.VMEM((2 * rows, width), bf16),
+            pltpu.VMEM((2 * rows, width), bf16),
+            pltpu.SemaphoreType.DMA((sems,)),
+            pltpu.SemaphoreType.DMA((sems,)),
+            pltpu.SemaphoreType.DMA((len(jobs) * 2 * layers,)),
         ],
-        out_specs=[
-            pl.BlockSpec((1, rows, tile), lambda i: (i // tiles, 0, i % tiles)),
-            pl.BlockSpec((rows, width), fixed),
-        ],
-        compiler_params=pltpu.CompilerParams(vmem_limit_bytes=LIMIT),
-    )(x, norm, weights, bias, cos, sin)
+        compiler_params=pltpu.CompilerParams(
+            collective_id=number, has_side_effects=True, vmem_limit_bytes=62 * 1024 * 1024
+        ),
+    )(*grads, q, keys, values, do, stats, row_dots, bias, cos, sin)
 
 
 def pad_to(values, axis, size):
@@ -1312,6 +1490,19 @@
 
 def round_up(size, step):
     return (size + step - 1) // step * step
+
+
+def tables(count, k, tokens_here, rows, head_size, grid_side):
+    columns = (count - 1.0) / grid_side
+    token = (k * tokens_here + jnp.arange(rows)).astype(jnp.float32)
+    live = jnp.logical_and(token >= 1.0, token < count)
+    row_id = jnp.floor((token - 0.5) / columns)
+    col_id = token - 1.0 - row_id * columns
+    angles = angle_table(jnp.where(live, row_id, 0.0), jnp.where(live, col_id, 0.0), head_size)
+    within = jnp.arange(rows)
+    seen = jnp.stack([within, within + tokens_here]).astype(jnp.float32) < count
+    seen = jnp.logical_and(seen, within < tokens_here)
+    return angles, jnp.where(seen, 0.0, -1e30).astype(jnp.float32).reshape(-1, 1)
 
 
 def image_per_chip(
@@ -1348,57 +1539,39 @@
     hidden_size = 2 * hidden_here
     score_scale = 1.0 / math.sqrt(head_size)
 
-    heads_flat = jnp.concatenate([head_biases, head_gain[None]], axis=0).reshape(-1, 128)
-    head_rows = heads_flat.shape[0]
-    vectors = jnp.concatenate([norm_gains, width_biases, heads_flat], axis=0)
-    vectors = pad_to(vectors, 0, 16)
+    padded = round_up(rows, 16)
+    heads_own = jnp.concatenate([head_biases, head_gain[None]], axis=0)
+    spot = jnp.zeros((4, heads_here, head_size), bf16)
+    spot = lax.dynamic_update_slice(spot, heads_own, (0, 0, s * dims_here)).reshape(4, -1)
+    width_own = jnp.concatenate([norm_gains, width_biases], axis=0)
+    lane_at = s * width_own.shape[1] - y * spot.shape[1]
+    inside = both(lane_at >= 0, lane_at < spot.shape[1])
+    width_own = jnp.where(inside, width_own, jnp.zeros_like(width_own))
+    at = jnp.where(inside, lane_at, 0)
+    lanes_own = lax.dynamic_update_slice(jnp.zeros((6, spot.shape[1]), bf16), width_own, (0, at))
+    vectors = pad_to(jnp.concatenate([spot, lanes_own], axis=0), 0, 16)
     hidden_vectors = jnp.concatenate([hidden_biases, hidden_gain[None]], axis=0)
     hidden_vectors = pad_to(pad_to(hidden_vectors, 1, hidden_here), 0, 16)
     gate_pad = pad_to(gate_up, 2, hidden_here)
     down_pad = pad_to(down_weight, 0, hidden_here)
-
-    jobs = (
-        (0, 0, ROW, 64), (0, 1, ROW, 64), (0, 2, ROW, 64), (1, None, COL, 0),
-        (2, None, COL, 256), (3, 0, ROW, 64), (3, 1, ROW, 64), (4, None, COL, hidden_here // 2),
+    swaps = []
+    for layer in range(layers):
+        swaps += [(4 * layer + 1, 4 * layer + 2), (4 * layer + 2, 4 * layer + 1)]
+    (
+        vec_full, qkv_full, out_full, gate_full, down_full, hidden_full,
+        token_block, first_in, queries, keys, values, mixed, stats, vec, count,
+    ) = front(
+        layers, 0, head_size, 32, vectors, qkv_weight, out_weight, gate_pad, down_pad,
+        pad_to(tokens, 1, padded), valid_tokens, hidden_vectors,
     )
-    (
-        qkv_full, vector_full, out_full, gate_full, down_full,
-        token_block, cot_block, valid_both, place_both, hidden_full,
-    ) = gather(
-        layers, 0, jobs, (qkv_weight, vectors, out_weight, gate_pad, down_pad),
-        (tokens, cotangent, valid_tokens, places), (hidden_vectors,),
-    )
-    norm_scale = vector_full[0:2].astype(f32)
-    width_bias = vector_full[2:6].astype(f32)
-    head_part = jnp.stack([vector_full[6 : 6 + head_rows], vector_full[22 : 22 + head_rows]])
-    head_part = head_part.reshape(2, head_rows, shards, 128).transpose(0, 2, 1, 3)
-    head_part = head_part.reshape(2, shards, 4, heads_here, dims_here).transpose(2, 0, 3, 1, 4)
-    head_part = head_part.reshape(4, heads * head_size).astype(f32)
+    cot_own = lax.dynamic_index_in_dim(cotangent, y, 0, keepdims=False)
+    cot_own = pad_to(cot_own, 0, padded)
+    cot_other = lax.ppermute(cot_own, (SHARD, CTX), swaps)
+    cot_block = jnp.where(k == x, cot_own, cot_other)
+    head_part, norm_scale, width_bias = vec[0:4], vec[4:6], vec[6:10]
     hidden_part = jnp.concatenate([hidden_full[0, :4], hidden_full[1, :4]], axis=1).astype(f32)
-
-    padded = round_up(rows, 16)
-    token_block = pad_to(token_block, 0, padded)
-    cot_block = pad_to(cot_block, 0, padded)
     token_rows = token_block.astype(f32)
     cot_rows = cot_block.astype(f32)
-    valid_row = lax.dynamic_index_in_dim(valid_both, y, 0, keepdims=False)
-    row_ids = pad_to(lax.dynamic_index_in_dim(place_both[0], y, 0, keepdims=False), 0, padded)
-    col_ids = pad_to(lax.dynamic_index_in_dim(place_both[1], y, 0, keepdims=False), 0, padded)
-    key_bias = jnp.where(pad_to(valid_row.reshape(2, rows), 1, padded) > 0, 0.0, -1e30)
-    key_bias = key_bias.astype(f32).reshape(1, 2 * padded)
-    angles = angle_table(row_ids, col_ids, head_size)
-    tile = 512
-    cos, sin = [jnp.tile(turn(angles), (1, tile // head_size)) for turn in (jnp.cos, jnp.sin)]
-    norm_one = jnp.stack([norm_scale[0], width_bias[0]])
-    qkv_bias = jnp.stack([head_part[0], jnp.zeros_like(head_part[0]), head_part[1]])[:, None]
-    qkv, first_in = project(token_block, norm_one, qkv_full, qkv_bias, cos, sin, head_size, tile)
-    pairs = [(i, i ^ 1) for i in range(shards)]
-    own = qkv[1:]
-    other = lax.ppermute(own, SHARD, pairs)
-    halves = jnp.stack([jnp.where(k == 0, own, other), jnp.where(k == 0, other, own)], axis=1)
-    keys = halves[0].reshape(2 * padded, width)
-    values = halves[1].reshape(2 * padded, width)
-    mixed, stats = mix_forward(qkv[0], keys, values, key_bias, head_size)
     mix_hat, spread_mix = standardize(mixed)
     mix_in = (mix_hat * head_part[3] + head_part[2]).astype(bf16)
     branch = jnp.dot(mix_in, out_full, preferred_element_type=f32)
@@ -1430,12 +1603,8 @@
         bf16
     )
     d_up = (d_hidden * silu_gate).astype(bf16)
-    g_gate_up = jnp.stack(
-        [
-            jnp.einsum("td,tf->df", second_in, d_gate, preferred_element_type=f32).astype(bf16),
-            jnp.einsum("td,tf->df", second_in, d_up, preferred_element_type=f32).astype(bf16),
-        ]
-    )
+    g_gate = jnp.einsum("td,tf->df", second_in, d_gate, preferred_element_type=f32).astype(bf16)
+    g_up = jnp.einsum("td,tf->df", second_in, d_up, preferred_element_type=f32).astype(bf16)
     d_second = jnp.einsum("tf,df->td", d_gate, gate_full[0], preferred_element_type=f32)
     d_second = d_second + jnp.einsum("tf,df->td", d_up, gate_full[1], preferred_element_type=f32)
     d_resid = cot_rows + norm_back(d_second * norm_scale[1], normed_two, spread_two)
@@ -1445,31 +1614,21 @@
     d_mixed = norm_back(d_mix_in * head_part[3], mix_hat, spread_mix).astype(bf16)
     row_dots = jnp.sum((d_mixed.astype(f32) * mixed).reshape(padded, heads // 2, 2, head_size), axis=-1)
     row_dots = row_dots.transpose(1, 2, 0)
-    d_query, d_keys, d_values = mix_backward(
-        qkv[0], keys, values, d_mixed, stats, row_dots, key_bias.reshape(-1, 1), head_size
+    angles, key_bias = tables(count[0, 0], k, rows, padded, head_size, 32)
+    cos, sin = [jnp.tile(turn(angles), (1, 2)) for turn in (jnp.cos, jnp.sin)]
+    grad_jobs = (
+        (0, None, COL, hidden_here // 2), (1, None, ROW, 64), (2, None, ROW, 64), (3, None, COL, 256),
     )
-
-    def pair_sum(parts):
-        mine = lax.dynamic_slice_in_dim(parts, k * padded, padded, axis=0)
-        yours = lax.dynamic_slice_in_dim(parts, (1 - k) * padded, padded, axis=0)
-        return mine.astype(f32) + lax.ppermute(yours, SHARD, pairs).astype(f32)
-
-    cos, sin = jnp.cos(angles), jnp.sin(angles)
-
-    def turn_back(values):
-        values = values.reshape(padded, heads, head_size)
-        turned = values * cos[:, None] - turn_half(values) * sin[:, None]
-        return turned.reshape(padded, width).astype(bf16)
-
-    d_query_low = turn_back(d_query)
-    d_key_low = turn_back(pair_sum(d_keys))
-    d_value_low = pair_sum(d_values).astype(bf16)
-    g_qkv = jnp.stack(
-        [
-            jnp.einsum("tn,tm->nm", first_in, part, preferred_element_type=f32).astype(bf16)
-            for part in (d_query_low, d_key_low, d_value_low)
-        ]
+    (
+        down_piece, gate_piece, up_piece, out_piece, d_query_low, d_key_low, d_value_low,
+    ) = back(
+        layers, 1, head_size, grad_jobs, (g_down.astype(bf16), g_gate, g_up, g_out.astype(bf16)),
+        queries, keys, values, d_mixed, stats, row_dots, key_bias, cos, sin,
     )
+    g_query, g_key, g_value = [
+        jnp.einsum("tn,tm->nm", first_in, part, preferred_element_type=f32).astype(bf16)
+        for part in (d_query_low, d_key_low, d_value_low)
+    ]
     d_first = jnp.einsum("tm,nm->tn", d_query_low, qkv_full[0], preferred_element_type=f32)
     d_first = d_first + jnp.einsum("tm,nm->tn", d_key_low, qkv_full[1], preferred_element_type=f32)
     d_first = d_first + jnp.einsum(
@@ -1497,12 +1656,9 @@
         ]
     ).reshape(-1, 128)
     vector_grads = pad_to(vector_grads, 0, round_up(vector_grads.shape[0], 16))
-    grad_jobs = (
-        (0, None, COL, hidden_here // 2), (1, 0, ROW, 64), (1, 1, ROW, 64), (2, None, COL, 256),
-        (3, 0, ROW, 64), (3, 1, ROW, 64), (3, 2, ROW, 64),
-    )
-    down_piece, gate_piece, out_piece, qkv_piece, vector_grads, result, d_tokens = reduce_grads(
-        layers, 1, grad_jobs, (g_down.astype(bf16), g_gate_up, g_out.astype(bf16), g_qkv),
+    late_jobs = ((0, None, ROW, 64), (1, None, ROW, 64), (2, None, ROW, 64))
+    query_piece, key_piece, value_piece, vector_grads, result, d_tokens = reduce_grads(
+        layers, 2, late_jobs, (g_query, g_key, g_value),
         vector_grads, (result[:rows], d_tokens[:rows].astype(bf16)),
     )
     vector_grads = vector_grads.reshape(-1)
@@ -1520,13 +1676,13 @@
     return (
         result,
         d_tokens.astype(f32),
-        qkv_piece,
+        jnp.stack([query_piece, key_piece, value_piece]),
         head_sums[:3],
         head_sums[3],
         out_piece,
         width_sums[:2],
         width_sums[2:],
-        gate_piece[:, :, :real_here],
+        jnp.stack([gate_piece[:, :real_here], up_piece[:, :real_here]]),
         hidden_sums[:3],
         hidden_sums[3],
         down_piece[:real_here],

time: 616 us -> 556 us (0.903)
  other arithmetic: 61.3 us -> 26.6 us
  local copies, waits for them, and re-layouts: 72.9 us -> 45.3 us
  matrix products: 76.8 us -> 89.1 us
    pallas_call x1, Pallas kernels: 185 us -> 105 us  [reduce_grads(): pl.pallas_call(functools.partial(reduce_kernel, layers, jobs, len(grads),...]
    pallas_call x4 -> x2, Pallas kernels: 207 us -> 281 us  [the longest x1 152 us: front(): pl.pallas_call(functools.partial(front_kernel, layers, head_size, grid_si...]
    another operation x8 -> x3, other arithmetic: 20.7 us -> 2.47 us  [the longest x1 10.2 us: image_per_chip(): jnp.stack([jnp.einsum('td,tf->df', second_in, d_gate, preferred_element_t...]
    mul x5 -> x0, local copies, waits for them, and re-layouts: 11.6 us -> none  [the longest x4 11.5 us: turn_back(): turned = values * cos[:, None] - turn_half(values) * sin[:, None]]
    reduce_sum x4 -> x5, other arithmetic: 16.3 us -> 12.5 us  [column_sum(): return jnp.sum(values.astype(jnp.float32), axis=0)]
    unnamed x119 -> x104, local copies, waits for them, and re-layouts: 23.4 us -> 20.3 us
  transfers between devices with their start and end apart: 3 -> 1, of which waited for: 0 -> 0; matrix products, arithmetic and copies ran while one was open for 10% -> 9% of each run, Pallas kernels for 0% -> 27%
where the time goes in v2:
time: 556 us; the launch traced here: 551 us
  Pallas kernels  386 us (69%)
  matrix products  89.1 us (16%)
  local copies, waits for them, and re-layouts  45.3 us (8%)
  other arithmetic  26.6 us (5%)
    pallas_call x1, Pallas kernels, front(): pl.pallas_call(functools.partial(front_kernel, layers, head_size, grid_si...  152 us
    pallas_call x1, Pallas kernels, back(): pl.pallas_call(functools.partial(back_kernel, layers, head_size, jobs, le...  130 us
    pallas_call x1, Pallas kernels, reduce_grads(): pl.pallas_call(functools.partial(reduce_kernel, layers, jobs, len(grads),...  105 us
    unnamed x104, local copies, waits for them, and re-layouts  20.3 us
    reduce_sum x5, other arithmetic, column_sum(): return jnp.sum(values.astype(jnp.float32), axis=0)  12.5 us
  transfers between devices with their start and end apart: 1, of which 0 were waited for; matrix products, arithmetic and copies ran while one was open for 9% of the time, Pallas kernels for 27%

profile of v2, /device:TPU:0, one launch (start us, length us, event | category | flops | bytes accessed | tf_op | source)
XLA Modules:
  0.0 551.4 jit_solution(16447823872545620129)
XLA Ops:
  0.6 3.8 constant_dynamic-slice_fusion.3
  6.9 1.8 collective-permute-start
  13.1 1.5 pad.35.refs_5_
  15.3 151.6 %shard_map.220 = (bf16[128,1024]{1,0:T(8,128)(2,1)}, bf16[3,1024,1024]{2,1,0:T(8,128)(2,1)}, bf16[1024,1024]{1,0:T(8,128)(2,1)}, bf16[2,1024,2816]{2,1,0:T(8,128...) custom-call(bf16[16,512]{1,0:T(8,128)(2,1)} %fusion.40.refs_0_, ...), custom_call_target="tpu_custom_call" | custom-call | tf_op jit(solution)/shard_map/pallas_call | solution.py:1347
  169.2 1.8 reduce_sum.279
  177.5 3.7 fusion.53
  182.1 6.3 %fusion.7 = f32[528,2816]{1,0:T(8,128)S(1)} fusion(bf16[528,1024]{1,0:T(8,128)(2,1)S(1)} %add_convert_fusion.1, bf16[2,1024,2816]{2,1,0:T(8,128)(2,1)} %get-tuple-element.44), kind=kOutput, calls=%fused_computation.17 | convolution fusion | flops 3045064704 | bytes 12795904 | tf_op jit(solution)/shard_map/dot_general | solution.py:1581
  188.4 11.0 %fusion.51 = (f32[528]{0:T(1024)S(1)}, f32[528,2816]{1,0:T(8,128)S(1)}, f32[528,2816]{1,0:T(8,128)}) fusion(f32[2816]{0:T(1024)S(1)} %get-tuple-element.108, f32[528,2816]{1,0:T(8,128)S(1)} %fusion.7, f32[2816]{0:T(1024)S(1)} %get-tuple-element.109, bf16[528,1024]{1,0:T(8,128)(2,1)S(1)} %add_convert_fusion.1, bf16[2,1024,2816]{2,1,0:T(8,128)(2,1)} %get-tuple-element.44), kind=kOutput, calls=%fused_computation.165 | convolution fusion | flops 3056958976 | bytes 24715328 | tf_op jit(solution)/shard_map/dot_general | solution.py:1582
  200.3 1.6 copy-done
  201.9 7.4 %fusion.48 = f32[528,1024]{1,0:T(8,128)S(1)} fusion(bf16[2816,1024]{1,0:T(8,128)(2,1)} %get-tuple-element.46, f32[528,2816]{1,0:T(8,128)} %copy-done, f32[2816]{0:T(1024)S(1)} %get-tuple-element.107, f32[2816]{0:T(1024)S(1)} %get-tuple-element.106, f32[528]{0:T(1024)S(1)} %add_rsqrt_fusion.1, f32[528]{0:T(1024)S(1)} %broadcast_multiply_fusion.5), kind=kOutput, calls=%fused_computation.162 | convolution fusion | flops 3052498944 | bytes 13904000 | tf_op jit(solution)/shard_map/dot_general | solution.py:1593
  209.3 1.5 fusion.19.refs_4_
  212.4 9.4 %multiply_reduce_fusion = (f32[2816]{0:T(1024)S(1)}, f32[528]{0:T(1024)S(1)}, f32[528]{0:T(1024)S(1)}, f32[2816]{0:T(1024)S(1)}, f32[528,2816]{1,0:T(8,128)}) fusion(f32[528,2816]{1,0:T(8,128)S(1)} %copy-done.1, f32[528]{0:T(1024)S(1)} %add_rsqrt_fusion.1, f32[528]{0:T(1024)S(1)} %broadcast_multiply_fusion.5, f32[2816]{0:T(1024)S(1)} %get-tuple-element.106, ...), kind=kOutput, calls=%fused_computation | convolution fusion | flops 3058439680 | bytes 18785536 | tf_op jit(solution)/shard_map/td,fd->tf/dot_general | solution.py:1597
  221.8 7.0 %convolution_convert_fusion.2.refs_0_ = bf16[2816,1024]{1,0:T(8,128)(2,1)} fusion(bf16[528,1024]{1,0:T(8,128)(2,1)S(1)} %get-tuple-element.116, f32[528,2816]{1,0:T(8,128)S(1)} %copy-done.1, f32[2816]{0:T(1024)S(1)} %get-tuple-element.107, f32[2816]{0:T(1024)S(1)} %get-tuple-element.106, f32[528]{0:T(1024)S(1)} %add_rsqrt_fusion.1, ...), kind=kOutput, calls=%fused_computation.21 | convolution fusion | flops 3055382528 | bytes 12822656 | tf_op jit(solution)/shard_map/tf,td->fd/dot_general | solution.py:1596
  228.8 8.2 %convert_reduce_fusion = (f32[2816]{0:T(1024)S(1)}, bf16[528,2816]{1,0:T(8,128)(2,1)S(1)}, f32[2816]{0:T(1024)S(1)}, bf16[528,2816]{1,0:T(8,128)(2,1)}) fusion(f32[528,2816]{1,0:T(8,128)S(1)} %bitcast.89, f32[2816]{0:T(1024)S(1)} %get-tuple-element.109, f32[528]{0:T(1024)S(1)} %broadcast_multiply_fusion.3, f32[528]{0:T(1024)S(1)} %add_rsqrt_fusion.1, ...), kind=kLoop, calls=%fused_computation.1 | loop fusion | flops 38652416 | bytes 29801728 | tf_op jit(solution)/shard_map/reduce_sum | solution.py:60
  237.1 5.5 fusion.1
  242.5 6.3 %multiply_reduce_fusion.5 = (f32[1024]{0:T(1024)S(1)}, f32[528]{0:T(1024)S(1)}, f32[528]{0:T(1024)S(1)}, f32[1024]{0:T(1024)S(1)}, f32[528,1024]{1,0:T(8,128)S(1)}) fusion(f32[528,1024]{1,0:T(8,128)S(1)} %get-tuple-element.142, f32[528]{0:T(1024)S(1)} %add_rsqrt_fusion.2, f32[528]{0:T(1024)S(1)} %broadcast_multiply_fusion.13, f32[1024]{0:T(1024)S(1)} %bitcast.102, ...), kind=kOutput, calls=%fused_computation.40 | convolution fusion | flops 3050468352 | bytes 15249664 | tf_op jit(solution)/shard_map/tf,df->td/dot_general | solution.py:1608
  251.8 1.9 multiply_reduce_fusion.7
  253.8 3.4 convolution_convert_fusion.6.refs_3_
  257.1 6.6 %convolution_convert_fusion.1.refs_1_ = bf16[1024,2816]{1,0:T(8,128)(2,1)} fusion(bf16[528,1024]{1,0:T(8,128)(2,1)S(1)} %copy-done.16, bf16[528,2816]{1,0:T(8,128)(2,1)S(1)} %copy-done.12), kind=kOutput, calls=%fused_computation.20 | convolution fusion | flops 3047948288 | bytes 9822208 | tf_op jit(solution)/shard_map/td,tf->df/dot_general | solution.py:1606
  263.8 6.6 %convolution_convert_fusion.refs_2_ = bf16[1024,2816]{1,0:T(8,128)(2,1)} fusion(bf16[528,1024]{1,0:T(8,128)(2,1)S(1)} %copy-done.16, bf16[528,2816]{1,0:T(8,128)(2,1)S(1)} %get-tuple-element.112), kind=kOutput, calls=%fused_computation.19 | convolution fusion | flops 3047948288 | bytes 9822208 | tf_op jit(solution)/shard_map/td,tf->df/dot_general | solution.py:1607
  270.4 2.5 convert_multiply_fusion
  272.9 2.1 copy.33
  275.8 129.7 %shard_map.221 = (f32[1408,128]{1,0:T(8,128)}, f32[128,1408]{1,0:T(8,128)}, f32[128,1408]{1,0:T(8,128)}, f32[512,128]{1,0:T(8,128)}, bf16[528,1024]{1,0:T(8,128)...) custom-call(bf16[2816,1024]{1,0:T(8,128)(2,1)} %convolution_convert_fusion.2.refs_0_, ...), custom_call_target="tpu_custom_call" | custom-call | tf_op jit(solution)/shard_map/pallas_call | solution.py:1463
  405.5 1.6 convert_reduce_fusion.6
  408.5 3.2 convolution_convert_fusion.5.refs_0_
  411.7 3.2 convolution_convert_fusion.3.refs_2_
  414.9 3.2 convolution_convert_fusion.4.refs_1_
  421.2 2.0 fusion.49
  425.5 105.1 %shard_map.222 = (f32[128,512]{1,0:T(8,128)}, f32[128,512]{1,0:T(8,128)}, f32[128,512]{1,0:T(8,128)}, f32[176,128]{1,0:T(8,128)}, bf16[2,516,1024]{2,1,0:T(8,128)(2,1)}, /*index=5*/bf16[2,516,1024]{2,1,0:T(8,128)(2,1)}) custom-call(bf16[1024,1024]{1,0:T(8,128)(2,1)} %convolution_convert_fusion.5.refs_0_, ...), custom_call_target="tpu_custom_call" | custom-call | tf_op jit(solution)/shard_map/pallas_call | solution.py:1080
  538.0 2.1 copy.39
  540.1 5.2 copy.37
  545.4 4.2 copy.38
  (183 shorter events, 38.4 us)
Async XLA Ops:
  4.4 4.3 copy-start.29
  4.4 4.4 copy-start.28
  4.5 4.4 copy-start.30
  4.5 4.6 copy-start.27
  4.5 5.3 copy-start.22
  4.9 5.6 %copy-start.20 = (bf16[2,128,1365]{1,0,2:T(2,128)(2,1)S(1)}, bf16[2,128,1365]{1,0,2:T(2,128)(2,1)}, u32[]{:S(2)}) copy-start(bf16[2,128,1365]{1,0,2:T(2,128)(2,1)} %param.23) | copy-start | bytes 2096644
  6.9 5.5 %copy-start.14 = (bf16[2,516,1024]{2,0,1:T(2,128)(2,1)S(1)}, bf16[2,516,1024]{2,0,1:T(2,128)(2,1)}, u32[]{:S(2)}) copy-start(bf16[2,516,1024]{2,0,1:T(2,128)(2,1)} %param.14) | copy-start | bytes 6340612
  6.9 203.9 %collective-permute-start = (bf16[528,1024]{1,0:T(8,128)(2,1)}, bf16[528,1024]{1,0:T(8,128)(2,1)}, u32[]{:S(2)}, u32[]{:S(2)}) collective-permute-start(bf16[528,1024]{1,0:T(8,128)(2,1)} %pad.38), channel_id=1, source_target_pairs={{2,4},{4,2},{10,12},{12,10},{18,20},{20,18},{26,28},{28,26},{3,5},... | collective-permute-start | bytes 3244040 | tf_op jit(solution)/shard_map/ppermute | solution.py:1569
  166.9 4.1 copy-start.2
  171.4 6.1 %copy-start.4 = (bf16[528,1024]{1,0:T(8,128)(2,1)S(1)}, bf16[528,1024]{1,0:T(8,128)(2,1)}, u32[]{:S(2)}) copy-start(bf16[528,1024]{1,0:T(8,128)(2,1)} %get-tuple-element.40) | copy-start | bytes 3244036
  182.1 6.3 %copy-start.15 = (bf16[528,1024]{1,0:T(8,128)(2,1)}, bf16[528,1024]{1,0:T(8,128)(2,1)S(1)}, u32[]{:S(2)}) copy-start(bf16[528,1024]{1,0:T(8,128)(2,1)S(1)} %add_convert_fusion.1) | copy-start | bytes 3244036
  188.3 11.0 %copy-start.10 = (f32[528,2816]{1,0:T(8,128)}, f32[528,2816]{1,0:T(8,128)S(1)}, u32[]{:S(2)}) copy-start(f32[528,2816]{1,0:T(8,128)S(1)} %fusion.7) | copy-start | bytes 17842180
  201.9 8.9 %copy-start.7 = (bf16[1,516,1024]{2,1,0:T(8,128)(2,1)S(1)}, bf16[1,516,1024]{2,1,0:T(8,128)(2,1)}, u32[]{:S(2)}) copy-start(bf16[1,516,1024]{2,1,0:T(8,128)(2,1)} %copy-done.6) | copy-start | bytes 3170308
  212.4 16.4 %slice-start = ((s8[5947392]{0:T(1024)(128)(4,1)}), s8[4194304]{0:T(1024)(128)(4,1)S(1)}, s32[]{:S(2)}) async-start(s8[5947392]{0:T(1024)(128)(4,1)} %bitcast.88), calls=%async_computation | async-start | bytes 8388608
  212.4 16.4 %slice-start.2 = ((s8[5947392]{0:T(1024)(128)(4,1)}), s8[4194304]{0:T(1024)(128)(4,1)S(1)}, s32[]{:S(2)}) async-start(s8[5947392]{0:T(1024)(128)(4,1)} %bitcast.90), calls=%async_computation.2 | async-start | bytes 8388608
  221.8 7.0 %slice-start.1 = ((s8[5947392]{0:T(1024)(128)(4,1)}), s8[1753088]{0:T(1024)(128)(4,1)S(1)}, s32[]{:S(2)}) async-start(s8[5947392]{0:T(1024)(128)(4,1)} %bitcast.88), calls=%async_computation.1 | async-start | bytes 3506176
  221.8 7.0 %slice-start.3 = ((s8[5947392]{0:T(1024)(128)(4,1)}), s8[1753088]{0:T(1024)(128)(4,1)S(1)}, s32[]{:S(2)}) async-start(s8[5947392]{0:T(1024)(128)(4,1)} %bitcast.90), calls=%async_computation.3 | async-start | bytes 3506176
  237.1 5.5 copy-start.12
  249.7 4.0 copy-start.8
  253.7 3.4 copy-start.16
  408.5 3.2 copy-start.17
  411.7 3.2 copy-start.35
  411.7 6.3 %slice-start.4 = ((s8[6291456]{0:T(1024)(128)(4,1)}), s8[4194304]{0:T(1024)(128)(4,1)S(1)}, s32[]{:S(2)}) async-start(s8[6291456]{0:T(1024)(128)(4,1)} %bitcast.94), calls=%async_computation.4 | async-start | bytes 8388608
  414.9 3.2 slice-start.5
  425.5 111.4 %copy-start.21 = (f32[1408,128]{1,0:T(8,128)S(1)}, f32[1408,128]{1,0:T(8,128)}, u32[]{:S(2)}) copy-start(f32[1408,128]{1,0:T(8,128)} %get-tuple-element.65) | copy-start | bytes 2162692
  530.5 7.3 %copy-start.19 = (f32[128,1408]{1,0:T(8,128)S(1)}, f32[128,1408]{1,0:T(8,128)}, u32[]{:S(2)}) copy-start(f32[128,1408]{1,0:T(8,128)} %get-tuple-element.63) | copy-start | bytes 2162692
  530.5 7.3 %copy-start.18 = (f32[128,1408]{1,0:T(8,128)S(1)}, f32[128,1408]{1,0:T(8,128)}, u32[]{:S(2)}) copy-start(f32[128,1408]{1,0:T(8,128)} %get-tuple-element.64) | copy-start | bytes 2162692
  540.1 5.3 copy-start.13
  545.3 4.2 copy-start.24
  545.3 4.2 copy-start.25
  545.3 4.2 copy-start.26
  545.4 5.1 copy-start.23
  (11 other events, 24.6 us)
